TPU v7x, 32 devices: a whole 2x2x4 slice. The times are simulated.
32 devices in a mesh: groups: 2 (over y), stn: 4 (over z), hour: 2 (over x), freq: 2 (over core).
Axes of the slice: x: 2, y: 2, z: 4, core: 2. Of those that a mesh axis runs over, the one named last changes fastest.
Arguments:
- spectra: bfloat16 [32, 512, 2, 512], P(('groups', 'hour'), 'stn', None, 'freq'), parts along dimension 0, may hold values from -6 to 6
- uptime: int32 [32, 512], P(('groups', 'hour'), 'stn'), parts along dimension 0, may hold values 0 or 1
- pair_blocks: int32 [16, 2], P('groups'), parts along dimension 0, may hold values from 0 to 63, as said below
Outputs:
- correlations: float32 [1024, 1024], P(('groups', 'stn', 'hour', 'freq')), parts along dimension 0
There are 2 independent parts, one for each index of `groups`. A program takes and returns all parts, laid end to end along the dimension named above; each array names one. Nothing has to cross between parts.
Inputs may be any that keep to these rules, and one draw needn't show every extreme that they name: `pair_blocks`: rows r * 2 to (r + 1) * 2 - 1 are the pair blocks read by station row r. Within one reader's rows all 4 block numbers differ; at most 2 of them lie among one owner's blocks (o * 16 to (o + 1) * 16 - 1), and for some owner exactly 2 do.
All inputs are finite; a program needn't handle non-finite values. No bound on the sum of `uptime` on one device may be relied on, other than what follows from the above.
Results may differ from a plain program's by a relative error of at most 0.0003.
Values may be sent and summed in bfloat16 or wider, within the bound.
No kernel may reach another device: no remote copies, remote signals or barrier semaphores. Data moves between devices by JAX's collectives and lax.ppermute only.
A program may use at most 128 MiB of HBM per device.

v0:
```python
import math

import jax
import jax.numpy as jnp
from jax import lax
from jax.sharding import PartitionSpec as P

L = 1024
SB = 8


def band_table(first, count, hour_total):
    half = L // 2
    freqs = first + jnp.arange(count, dtype=jnp.int32)
    lag_index = jnp.arange(L, dtype=jnp.int32)
    phase = freqs[:, None] * lag_index[None, :] % L
    angle = phase.astype(jnp.float32) * (2.0 * math.pi / L)
    weight = jnp.sin(math.pi * (freqs.astype(jnp.float32) + 0.5) / half) ** 2 / math.sqrt(
        hour_total * half
    )
    return jnp.concatenate(
        [jnp.cos(angle) * weight[:, None], -jnp.sin(angle) * weight[:, None]], axis=0
    )


def cross_of(grouped):
    block_total = grouped.shape[1]
    freq_loc = grouped.shape[5]
    first = grouped[:, :, 0]
    second = grouped[:, :, 1]
    real = jnp.einsum(
        "hksf,hktf->kstf", first[:, :, :, 0], second[:, :, :, 0], preferred_element_type=jnp.float32
    )
    real = real + jnp.einsum(
        "hksf,hktf->kstf", first[:, :, :, 1], second[:, :, :, 1], preferred_element_type=jnp.float32
    )
    imag = jnp.einsum(
        "hksf,hktf->kstf", first[:, :, :, 1], second[:, :, :, 0], preferred_element_type=jnp.float32
    )
    imag = imag - jnp.einsum(
        "hksf,hktf->kstf", first[:, :, :, 0], second[:, :, :, 1], preferred_element_type=jnp.float32
    )
    return jnp.concatenate([real, imag], axis=3).reshape(block_total * SB * SB, 2 * freq_loc)


def per_device(spectra, uptime, pair_blocks):
    hours_loc, stations_loc, _, freq_loc = spectra.shape
    readers = lax.axis_size("stn")
    me_row = lax.axis_index("stn")
    masked = jnp.where(uptime[:, :, None, None] > 0, spectra, jnp.zeros_like(spectra))
    reader_blocks = pair_blocks.shape[0] // readers
    wanted = pair_blocks.reshape(readers, 2 * reader_blocks)
    mine = lax.dynamic_index_in_dim(wanted, me_row, 0, keepdims=False)
    slot_station = (mine[:, None] * SB + jnp.arange(SB, dtype=jnp.int32)[None, :]).reshape(-1)
    start_fill = jnp.zeros((hours_loc, 2 * reader_blocks * SB, 2, freq_loc), jnp.bfloat16)
    piece = lax.all_gather(masked, "stn", axis=1, tiled=True)
    count = piece.shape[1]
    inside = (slot_station >= 0) & (slot_station < count)
    taken = jnp.take(piece, jnp.clip(slot_station, 0, count - 1), axis=1)
    chosen = jnp.where(inside[None, :, None, None], taken, start_fill)
    grouped = chosen.reshape(hours_loc, reader_blocks, 2, SB, 2, freq_loc)
    hour_total = hours_loc * lax.axis_size("hour")
    table = band_table(lax.axis_index("freq") * freq_loc, freq_loc, hour_total)
    cross = cross_of(grouped)
    return lax.psum_scatter(
        jnp.dot(cross, table, precision=lax.Precision.HIGHEST, preferred_element_type=jnp.float32),
        ("hour", "freq"),
        scatter_dimension=0,
        tiled=True,
    )


def solution(mesh):
    in_specs = (
        P(("groups", "hour"), "stn", None, "freq"),
        P(("groups", "hour"), "stn"),
        P("groups", None),
    )
    out_specs = P(("groups", "stn", "hour", "freq"), None)
    return jax.shard_map(
        per_device, mesh=mesh, in_specs=in_specs, out_specs=out_specs, check_vma=False
    )
```

profile of v0, /device:TPU:0, one launch (start us, length us, event | category | flops | bytes accessed | tf_op | source)
XLA Modules:
  0.0 146.1 jit_solution(11355466007284374681)
XLA Ops:
  6.5 0.0 all-gather.2.cloned.1.call-start
  6.5 0.7 broadcast_compare_fusion
  7.2 0.1 copy.31
  7.4 2.9 %copy_select_fusion = bf16[8,128,2,256]{3,0,2,1:T(8,128)(2,1)} fusion(bf16[8,128,2,256]{3,2,1,0:T(2,128)(2,1)} %param.3, pred[8,128]{0,1:T(8,128)(4,1)S(1)} %copy.31), kind=kLoop, calls=%fused_computation.20 | loop fusion | flops 524288 | bytes 2098176 | tf_op jit(solution)/shard_map/jit(_where)/select_n | solution.py:50
  10.2 0.0 all-gather.2.cloned.1.call-update
  10.3 0.0 reduce-scatter.2.cloned.1.call-start
  10.3 0.0 copy-done.2
  10.3 0.1 copy.29
  10.4 0.1 reshape.104
  10.5 0.1 mul.55
  10.6 0.1 copy.30
  10.7 0.1 add_clamp_fusion
  10.8 0.1 min.18
  10.9 0.1 compare_and_fusion.1
  11.0 5.7 %cosine_multiply_fusion = (f32[256,1024]{1,0:T(8,128)S(1)}, f32[256,1024]{1,0:T(8,128)}) fusion(f32[256]{0:T(256)S(1)} %multiply_multiply_fusion, s32[256]{0:T(256)S(1)} %iota_add_fusion.1), kind=kLoop, calls=%fused_computation.22 | loop fusion | flops 4456448 | bytes 2099200 | tf_op jit(solution)/shard_map/mul | solution.py:22
  16.7 77.2 %all-gather.2.cloned.1.call-done = bf16[8,512,2,256]{3,0,2,1:T(8,128)(2,1)} async-done(((bf16[8,128,2,256]{3,0,2,1:T(8,128)(2,1)}), bf16[8,512,2,256]{3,0,2,1:T(8,128)(2,1)}) %all-gather.2.cloned.1.call-update) | async-done | bytes 4194320 | tf_op jit(solution)/shard_map/all_gather | solution.py:56
  93.9 2.8 %gather_fusion = bf16[32,8,2,256]{3,1,2,0:T(8,128)(2,1)S(1)} fusion(bf16[8,512,2,256]{3,0,2,1:T(8,128)(2,1)} %all-gather.2.cloned.1.call-done, s32[1024]{0:T(1024)S(1)} %pad_clamp_fusion), kind=kCustom, calls=%fused_computation | custom fusion | bytes 524416 | tf_op jit(solution)/shard_map/jit(_take)/gather | solution.py:59
  96.6 3.6 %copy.34 = bf16[8,2,2,8,2,256]{3,0,5,1,4,2:T(8,128)(2,1)} copy(bf16[8,2,2,8,2,256]{5,0,4,3,2,1:T(8,128)(2,1)S(1)} %bitcast.33) | data formatting | bytes 524288 | tf_op jit(solution)/shard_map/jit(_take)/gather | solution.py:59
  100.2 2.7 %select_select_fusion = bf16[8,2,2,8,2,256]{3,0,5,1,4,2:T(8,128)(2,1)S(1)} fusion(bf16[8,2,2,8,2,256]{3,0,5,1,4,2:T(8,128)(2,1)} %copy.34, pred[2,2,8]{2,0,1:T(4,128)(4,1)S(1)} %get-tuple-element.12, pred[2,2,8]{2,0,1:T(4,128)(4,1)S(1)} %get-tuple-element.11), kind=kLoop, calls=%fused_computation.1 | loop fusion | flops 262144 | bytes 524352 | tf_op jit(solution)/shard_map/jit(_where)/select_n | solution.py:60
  102.9 0.3 slice_bitcast_fusion
  103.2 0.0 copy-start
  103.2 0.8 fusion.11
  104.0 2.1 %fusion.10 = f32[2,256,8,8]{3,2,1,0:T(8,128)} fusion(bf16[8,2,8,2,256]{2,0,4,1,3:T(8,128)(2,1)S(1)} %get-tuple-element.6, bf16[8,2,8,2,256]{2,0,4,1,3:T(8,128)(2,1)S(1)} %get-tuple-element.5), kind=kOutput, calls=%fused_computation.26 | convolution fusion | flops 524288 | bytes 2228224 | tf_op jit(solution)/shard_map/hksf,hktf->kstf/dot_general | solution.py:37
  106.1 0.0 copy-done
  106.1 2.2 %add_bitcast_fusion = f32[2,8,8,256]{1,2,3,0:T(8,128)} fusion(f32[2,256,8,8]{3,2,1,0:T(8,128)S(1)} %fusion.11, bf16[8,2,8,2,256]{2,0,4,1,3:T(8,128)(2,1)S(1)} %get-tuple-element.6, bf16[8,2,8,2,256]{2,0,4,1,3:T(8,128)(2,1)S(1)} %get-tuple-element.5), kind=kOutput, calls=%fused_computation.9 | convolution fusion | flops 557056 | bytes 4325376 | tf_op jit(solution)/shard_map/hksf,hktf->kstf/dot_general | solution.py:34
  108.3 2.2 %copy.39 = f32[2,8,8,256]{3,2,1,0:T(8,128)S(1)} copy(f32[2,8,8,256]{1,2,3,0:T(8,128)} %add_bitcast_fusion) | data formatting | bytes 262144 | tf_op jit(solution)/shard_map/add | solution.py:34
  110.4 4.0 %subtract_bitcast_fusion = f32[2,8,8,256]{1,2,3,0:T(8,128)} fusion(f32[2,256,8,8]{3,2,1,0:T(8,128)} %fusion.10, bf16[8,2,8,2,256]{2,0,4,1,3:T(8,128)(2,1)S(1)} %get-tuple-element.5, bf16[8,2,8,2,256]{2,0,4,1,3:T(8,128)(2,1)} %copy-done), kind=kOutput, calls=%fused_computation.8 | convolution fusion | flops 557056 | bytes 4325376 | tf_op jit(solution)/shard_map/hksf,hktf->kstf/dot_general | solution.py:40
  114.5 2.3 %copy.40 = f32[2,8,8,256]{3,2,1,0:T(8,128)S(1)} copy(f32[2,8,8,256]{1,2,3,0:T(8,128)} %subtract_bitcast_fusion) | data formatting | bytes 262144 | tf_op jit(solution)/shard_map/sub | solution.py:40
  116.8 0.0 copy-done.1
  116.8 2.1 %fusion = f32[128,1024]{1,0:T(8,128)} fusion(f32[128,512]{1,0:T(8,128)S(1)} %bitcast.34, f32[256,1024]{1,0:T(8,128)S(1)} %copy-done.1, f32[256,1024]{1,0:T(8,128)S(1)} %get-tuple-element.7), kind=kOutput, calls=%fused_computation.4 | convolution fusion | flops 805830656 | bytes 2883584 | tf_op jit(solution)/shard_map/dot_general | solution.py:66
  118.9 0.0 reduce-scatter.2.cloned.1.call-update
  118.9 20.3 %reduce-scatter.2.cloned.1.call-done = f32[32,1024]{1,0:T(8,128)} async-done(((f32[128,1024]{1,0:T(8,128)}), f32[32,1024]{1,0:T(8,128)}) %reduce-scatter.2.cloned.1.call-update) | async-done | bytes 131088 | tf_op jit(solution)/shard_map/reduce_scatter | solution.py:65
  (8 shorter events, 0.1 us)
Async XLA Ops:
  6.5 3.8 %copy-start.2 = (s32[8,2]{0,1:T(2,128)S(1)}, s32[8,2]{0,1:T(2,128)}, u32[]{:S(2)}) copy-start(s32[8,2]{0,1:T(2,128)} %param.5) | copy-start | bytes 196
  6.5 87.3 %all-gather.2.cloned.1.call-start = ((), (), s32[]{:S(2)}) async-start(), calls=%async_computation.1 | async-start | bytes 5242880 | tf_op jit(solution)/shard_map/all_gather | solution.py:56
  10.3 129.0 %reduce-scatter.2.cloned.1.call-start = ((), (), s32[]{:S(2)}) async-start(), calls=%async_computation.2 | async-start | bytes 655360 | tf_op jit(solution)/shard_map/reduce_scatter | solution.py:65
  103.2 2.9 %copy-start = (bf16[8,2,8,2,256]{2,0,4,1,3:T(8,128)(2,1)}, bf16[8,2,8,2,256]{2,0,4,1,3:T(8,128)(2,1)S(1)}, u32[]{:S(2)}) copy-start(bf16[8,2,8,2,256]{2,0,4,1,3:T(8,128)(2,1)S(1)} %get-tuple-element.6) | copy-start | bytes 393220
  114.5 2.3 %copy-start.1 = (f32[256,1024]{1,0:T(8,128)S(1)}, f32[256,1024]{1,0:T(8,128)}, u32[]{:S(2)}) copy-start(f32[256,1024]{1,0:T(8,128)} %get-tuple-element.8) | copy-start | bytes 3145732
Sparse Core Ops, SparseCore 0:
  10.4 83.4 all-gather.1
  119.0 20.1 reduce-scatter.1
where the time goes:
time: 146 us
  waiting for transfers between devices  97.5 us (67%)
  between operations  13.5 us (9%)
  other arithmetic  12.2 us (8%)
  local copies, waits for them, and re-layouts  11.6 us (8%)
  matrix products  11.2 us (8%)
    all_gather x1, waiting for transfers between devices, per_device(): piece = lax.all_gather(masked, 'stn', axis=1, tiled=True)  77.2 us
    reduce_scatter x1, waiting for transfers between devices, per_device(): lax.psum_scatter(jnp.dot(cross, table, precision=lax.Precision.HIGHEST, p...  20.3 us
    gather x2, local copies, waits for them, and re-layouts, per_device(): taken = jnp.take(piece, jnp.clip(slot_station, 0, count - 1), axis=1)  6.35 us
    mul x1, other arithmetic, band_table(): jnp.cos(angle) * weight[:, None]  5.7 us
    dot_general x1, matrix products, cross_of(): jnp.einsum('hksf,hktf->kstf', first[:, :, :, 0], second[:, :, :, 1], pref...  4.04 us
  transfers between devices with their start and end apart: 2, of which 2 were waited for; matrix products, arithmetic and copies ran while one was open for 4% of the time, Pallas kernels for 0%

commit v1 on v0

v1 whole, which is shorter than its diff:
```python
import functools
import math

import jax
import jax.numpy as jnp
from jax import lax
from jax.experimental import pallas as pl
from jax.experimental.pallas import tpu as pltpu
from jax.sharding import PartitionSpec as P

L = 1024
SB = 8
CAP = 2
LANES = 128


def exchange(x, axes, size, distance):
    return lax.ppermute(x, axes, [(i, i ^ distance) for i in range(size)])


def slots_kernel(readers, pairs_ref, uptime_ref, spectra_ref, *out_refs):
    me = lax.axis_index("stn")
    hours, stations = uptime_ref.shape
    freq_loc = spectra_ref.shape[3]
    owned = stations // SB
    reader_blocks = pairs_ref.shape[1] // readers
    rows = SB * 2
    up = uptime_ref[...].astype(jnp.float32).astype(jnp.bfloat16)
    for distance in range(readers):
        reader = me ^ distance
        slots = [jnp.int32(0)] * CAP
        found = jnp.int32(0)
        for entry in range(2 * reader_blocks):
            block = pairs_ref[entry % 2, reader * reader_blocks + entry // 2]
            mine = (block >= me * owned) & (block < (me + 1) * owned)
            for slot in range(CAP):
                slots[slot] = jnp.where(mine & (found == slot), block - me * owned, slots[slot])
            found = found + mine.astype(jnp.int32)
        for slot in range(CAP):
            base = slots[slot] * SB
            station = lax.broadcasted_iota(jnp.int32, (rows, stations), 1)
            row = lax.broadcasted_iota(jnp.int32, (rows, stations), 0)
            pick = (station == base + row // 2).astype(jnp.float32).astype(jnp.bfloat16)
            recorded = lax.dot_general(
                pick, up, (((1,), (1,)), ((), ())), preferred_element_type=jnp.float32
            )
            for hour in range(hours):
                values = spectra_ref[hour, pl.ds(base, SB)].astype(jnp.float32)
                values = values.reshape(rows, freq_loc)
                keep = jnp.broadcast_to(recorded[:, hour : hour + 1], (rows, freq_loc)) > 0
                out_refs[distance][slot, hour] = jnp.where(keep, values, 0.0).astype(jnp.bfloat16)


def cross_kernel(readers, parts, freq_parts, owned, pairs_ref, *refs):
    slot_refs, out_refs, blocks = refs[:readers], refs[readers : readers + parts], refs[-1]
    me = lax.axis_index("stn")
    mine = lax.axis_index("hour") * freq_parts + lax.axis_index("freq")
    reader_blocks = pairs_ref.shape[1] // readers
    _, chunks, hours, _, _ = blocks.shape
    wanted = [
        pairs_ref[entry % 2, me * reader_blocks + entry // 2] for entry in range(2 * reader_blocks)
    ]
    owners = [block // owned for block in wanted]
    for entry in range(2 * reader_blocks):
        slot = jnp.int32(0)
        for before in range(entry):
            slot = slot + (owners[before] == owners[entry]).astype(jnp.int32)
        slot = jnp.minimum(slot, CAP - 1)
        for distance in range(readers):

            @pl.when(owners[entry] == me ^ distance)
            def _(entry=entry, slot=slot, distance=distance):
                values = slot_refs[distance][slot].astype(jnp.float32)
                for chunk in range(blocks.shape[1]):
                    blocks[entry, chunk] = values[:, :, chunk * LANES : (chunk + 1) * LANES]

    part_rows = out_refs[0].shape[1] // SB
    for distance in range(parts):
        first_row = (mine ^ distance) * part_rows
        pair = first_row // SB
        station = first_row % SB
        for chunk in range(chunks):
            lanes = pl.ds(chunk * LANES, LANES)
            second = 2 * pair + 1
            second_re = [blocks[second, chunk, h, pl.ds(0, SB, stride=2)] for h in range(hours)]
            second_im = [blocks[second, chunk, h, pl.ds(1, SB, stride=2)] for h in range(hours)]
            for s in range(part_rows):
                real = jnp.zeros((SB, LANES), jnp.float32)
                imag = jnp.zeros((SB, LANES), jnp.float32)
                for h in range(hours):
                    first_re = blocks[2 * pair, chunk, h, pl.ds(2 * (station + s), 1)]
                    first_im = blocks[2 * pair, chunk, h, pl.ds(2 * (station + s) + 1, 1)]
                    real = real + first_re * second_re[h] + first_im * second_im[h]
                    imag = imag + first_im * second_re[h] - first_re * second_im[h]
                out_refs[distance][0, pl.ds(s * SB, SB), lanes] = real
                out_refs[distance][1, pl.ds(s * SB, SB), lanes] = imag


def table_kernel(hour_total, high_ref, low_ref):
    halves, twice, _ = high_ref.shape
    freq_loc = twice // 2
    half = L // 2
    turns = L // LANES
    sub = lax.broadcasted_iota(jnp.int32, (8, LANES), 0)
    lane = lax.broadcasted_iota(jnp.int32, (8, LANES), 1)
    steps = []
    for j in range(turns):
        turn = ((sub * j) % turns).astype(jnp.float32) * (2.0 * math.pi / turns)
        steps.append((jnp.cos(turn), jnp.sin(turn)))

    def rows(index, carry):
        c = index // (freq_loc // 8)
        r = index % (freq_loc // 8)
        freq = index * 8 + sub
        angle = ((freq * lane) % L).astype(jnp.float32) * (2.0 * math.pi / L)
        weight = jnp.sin(math.pi * (freq.astype(jnp.float32) + 0.5) / half) ** 2 / math.sqrt(
            hour_total * half
        )
        cos0 = jnp.cos(angle) * weight
        sin0 = jnp.sin(angle) * weight
        for j in range(turns):
            cj, sj = steps[j]
            lanes = pl.ds(j * LANES, LANES)
            for where, value in ((0, cos0 * cj - sin0 * sj), (freq_loc, -(sin0 * cj + cos0 * sj))):
                at = pl.ds(pl.multiple_of(where + r * 8, 8), 8)
                high = value.astype(jnp.bfloat16)
                high_ref[c, at, lanes] = high
                low_ref[c, at, lanes] = (value - high.astype(jnp.float32)).astype(jnp.bfloat16)
        return carry

    lax.fori_loop(0, halves * freq_loc // 8, rows, 0)


def lags_kernel(parts, freq_parts, high_ref, low_ref, *refs):
    part_refs, out_ref = refs[:parts], refs[-1]
    own = lax.axis_index("freq")
    total = None
    for c in range(freq_parts):
        cross = part_refs[c][...]
        for x in range(1, parts // freq_parts):
            cross = cross + part_refs[x * freq_parts + c][...]
        cross = jnp.concatenate([cross[0], cross[1]], axis=1)
        count = cross.shape[0]
        high = cross.astype(jnp.bfloat16)
        low = (cross - high.astype(jnp.float32)).astype(jnp.bfloat16)
        both = jnp.concatenate([high, low], axis=0)
        table = own ^ c
        by_high = jnp.dot(both, high_ref[table], preferred_element_type=jnp.float32)
        by_low = jnp.dot(high, low_ref[table], preferred_element_type=jnp.float32)
        term = by_high[:count] + (by_high[count:] + by_low)
        total = term if total is None else total + term
    out_ref[...] = total


def per_device(sizes, spectra, uptime, pair_blocks):
    readers, hour_parts, freq_parts = sizes
    hours, stations, _, freq_loc = spectra.shape
    parts = hour_parts * freq_parts
    reader_blocks = pair_blocks.shape[0] // readers
    part_pairs = reader_blocks * SB * SB // parts
    pairs = pair_blocks.T
    vmem = pl.BlockSpec(memory_space=pltpu.VMEM)
    smem = pl.BlockSpec(memory_space=pltpu.SMEM)
    limit = pltpu.CompilerParams(vmem_limit_bytes=32 * 1024 * 1024)

    slots = pl.pallas_call(
        functools.partial(slots_kernel, readers),
        out_shape=[jax.ShapeDtypeStruct((CAP, hours, 2 * SB, freq_loc), jnp.bfloat16)] * readers,
        in_specs=[smem, vmem, vmem],
        out_specs=[vmem] * readers,
        compiler_params=limit,
        name="slots",
    )(pairs, uptime, spectra)

    order = sorted(range(1, readers), key=lambda d: (d < readers // 2, d))
    arrived = [slots[0]] + [None] * (readers - 1)
    for distance in order:
        arrived[distance] = exchange(slots[distance], "stn", readers, distance)

    high, low = pl.pallas_call(
        functools.partial(table_kernel, hours * hour_parts),
        out_shape=[jax.ShapeDtypeStruct((freq_parts, 2 * freq_loc, L), jnp.bfloat16)] * 2,
        out_specs=[vmem] * 2,
        compiler_params=limit,
        cost_estimate=pl.CostEstimate(flops=20_000_000, bytes_accessed=4_000_000, transcendentals=0),
        name="band_table",
    )()

    cross = pl.pallas_call(
        functools.partial(cross_kernel, readers, parts, freq_parts, stations // SB),
        out_shape=[jax.ShapeDtypeStruct((2, part_pairs, freq_loc), jnp.float32)] * parts,
        in_specs=[smem] + [vmem] * readers,
        out_specs=[vmem] * parts,
        scratch_shapes=[pltpu.VMEM((2 * reader_blocks, freq_loc // LANES, hours, 2 * SB, LANES), jnp.float32)],
        compiler_params=limit,
        name="cross",
    )(pairs, *arrived)

    summed = [cross[0]] + [
        exchange(cross[distance], ("hour", "freq"), parts, distance) for distance in range(1, parts)
    ]

    return pl.pallas_call(
        functools.partial(lags_kernel, parts, freq_parts),
        out_shape=jax.ShapeDtypeStruct((part_pairs, L), jnp.float32),
        in_specs=[vmem] * (2 + parts),
        out_specs=vmem,
        compiler_params=limit,
        name="lags",
    )(high, low, *summed)


def solution(mesh):
    sizes = (mesh.shape["stn"], mesh.shape["hour"], mesh.shape["freq"])
    in_specs = (
        P(("groups", "hour"), "stn", None, "freq"),
        P(("groups", "hour"), "stn"),
        P("groups", None),
    )
    out_specs = P(("groups", "stn", "hour", "freq"), None)
    return jax.shard_map(
        functools.partial(per_device, sizes),
        mesh=mesh,
        in_specs=in_specs,
        out_specs=out_specs,
        check_vma=False,
    )
```

time: 146 us -> 29.3 us (0.20)
  waiting for transfers between devices: 97.5 us -> 10.3 us
  between operations: 13.5 us -> 0.06 us
  other arithmetic: 12.2 us -> 0 us
  matrix products: 11.2 us -> 0 us
  local copies, waits for them, and re-layouts: 11.6 us -> 2.59 us
  Pallas kernels: 0 us -> 8.53 us
  starting transfers between devices: 0.04 us -> 7.61 us
    all_gather x1 -> x0, waiting for transfers between devices: 77.2 us -> none  [per_device(): piece = lax.all_gather(masked, 'stn', axis=1, tiled=True)]
    reduce_scatter x1 -> x0, waiting for transfers between devices: 20.3 us -> none  [per_device(): lax.psum_scatter(jnp.dot(cross, table, precision=lax.Precision.HIGHEST, p...]
    dot_general x5 -> x0, matrix products: 11.2 us -> none  [the longest x1 4.04 us: cross_of(): jnp.einsum('hksf,hktf->kstf', first[:, :, :, 0], second[:, :, :, 1], pref...]
    ppermute x0 -> x6, waiting for transfers between devices: none -> 10.3 us  [exchange(): return lax.ppermute(x, axes, [(i, i ^ distance) for i in range(size)])]
    pallas_call x0 -> x4, Pallas kernels: none -> 8.53 us  [the longest x1 5.08 us: per_device(): pl.pallas_call(functools.partial(table_kernel, hours * hour_parts), out_s...]
    ppermute x0 -> x6, starting transfers between devices: none -> 7.61 us  [exchange(): return lax.ppermute(x, axes, [(i, i ^ distance) for i in range(size)])]
    gather x2 -> x0, local copies, waits for them, and re-layouts: 6.35 us -> none  [per_device(): taken = jnp.take(piece, jnp.clip(slot_station, 0, count - 1), axis=1)]
    mul x2 -> x0, other arithmetic: 5.72 us -> none  [the longest x1 5.7 us: band_table(): jnp.cos(angle) * weight[:, None]]
  transfers between devices with their start and end apart: 2 -> 6, of which waited for: 2 -> 2; matrix products, arithmetic and copies ran while one was open for 4% -> 0% of each run, Pallas kernels for 0% -> 17%
where the time goes in v1:
time: 29.3 us; the launch traced here: 29.1 us
  waiting for transfers between devices  10.3 us (35%)
  Pallas kernels  8.53 us (29%)
  starting transfers between devices  7.61 us (26%)
  local copies, waits for them, and re-layouts  2.59 us (9%)
    ppermute x6, waiting for transfers between devices, exchange(): return lax.ppermute(x, axes, [(i, i ^ distance) for i in range(size)])  10.3 us
    ppermute x6, starting transfers between devices, exchange(): return lax.ppermute(x, axes, [(i, i ^ distance) for i in range(size)])  7.61 us
    pallas_call x1, Pallas kernels, per_device(): pl.pallas_call(functools.partial(table_kernel, hours * hour_parts), out_s...  5.08 us
    unnamed x6, local copies, waits for them, and re-layouts  2.59 us
    pallas_call x1, Pallas kernels, per_device(): pl.pallas_call(functools.partial(lags_kernel, parts, freq_parts), out_sha...  1.49 us
    pallas_call x1, Pallas kernels, per_device(): pl.pallas_call(functools.partial(slots_kernel, readers), out_shape=[jax.S...  0.99 us
    pallas_call x1, Pallas kernels, per_device(): pl.pallas_call(functools.partial(cross_kernel, readers, parts, freq_parts...  0.97 us
  transfers between devices with their start and end apart: 6, of which 2 were waited for; matrix products, arithmetic and copies ran while one was open for 0% of the time, Pallas kernels for 17%

profile of v1, /device:TPU:0, one launch (start us, length us, event | category | flops | bytes accessed | tf_op | source)
XLA Modules:
  0.0 29.1 jit_solution(14604004410698895215)
XLA Ops:
  0.0 0.0 copy-start
  0.0 1.2 %copy-done = bf16[8,128,2,256]{3,2,1,0:T(2,128)(2,1)S(1)} copy-done((bf16[8,128,2,256]{3,2,1,0:T(2,128)(2,1)S(1)}, bf16[8,128,2,256]{3,2,1,0:T(2,128)(2,1)}, u32[]{:S(2)}) %copy-start) | copy-done | bytes 1048600
  1.2 0.0 copy-start.1
  1.2 0.7 %copy-done.1 = s32[8,128]{1,0:T(8,128)S(1)} copy-done((s32[8,128]{1,0:T(8,128)S(1)}, s32[8,128]{1,0:T(8,128)}, u32[]{:S(2)}) %copy-start.1) | copy-done | bytes 4120
  1.9 0.0 copy-start.2
  1.9 0.7 %copy-done.2 = s32[8,2]{0,1:T(2,128)S(1)} copy-done((s32[8,2]{0,1:T(2,128)S(1)}, s32[8,2]{0,1:T(2,128)}, u32[]{:S(2)}) %copy-start.2) | copy-done | bytes 88
  2.6 1.0 %slots.1 = (bf16[2,8,16,256]{3,2,1,0:T(8,128)(2,1)S(1)}, bf16[2,8,16,256]{3,2,1,0:T(8,128)(2,1)S(1)}, bf16[2,8,16,256]{3,2,1,0:T(8,128)(2,1)S(1)}, bf16[2,8,16,256]{3,2,1,0:T(8,128)(2,1)S(1)}) custom-call(s32[2,8]{1,0:T(2,128)S(1)} %bitcast.1, s32[8,128]{1,0:T(8,128)S(1)} %copy-done.1, bf16[8,128,2,256]{3,2,1,0:T(2,128)(2,1)S(1)} %copy-done), custom_call_target="tpu_custom_call" | custom-call | tf_op jit(solution)/shard_map/slots/pallas_call | solution.py:166
  3.6 3.1 %collective-permute-start = (bf16[2,8,16,256]{3,2,1,0:T(8,128)(2,1)S(1)}, bf16[2,8,16,256]{3,2,1,0:T(8,128)(2,1)S(1)}, u32[]{:S(2)}, u32[]{:S(2)}) collective-permute-start(bf16[2,8,16,256]{3,2,1,0:T(8,128)(2,1)S(1)} %get-tuple-element.18), channel_id=1, source_target_pairs={{0,4},{4,0},{8,12},{12,8},{1,5},{5,1},{9,13},{13,9},{2,6},{6,2},{1... | collective-permute-start | bytes 393224 | tf_op jit(solution)/shard_map/ppermute | solution.py:18
  6.7 2.6 %collective-permute-start.1 = (bf16[2,8,16,256]{3,2,1,0:T(8,128)(2,1)S(1)}, bf16[2,8,16,256]{3,2,1,0:T(8,128)(2,1)S(1)}, u32[]{:S(2)}, u32[]{:S(2)}) collective-permute-start(bf16[2,8,16,256]{3,2,1,0:T(8,128)(2,1)S(1)} %get-tuple-element.19), channel_id=1, source_target_pairs={{0,8},{4,12},{8,0},{12,4},{1,9},{5,13},{9,1},{13,5},{2,10},{6,14},... | collective-permute-start | bytes 393224 | tf_op jit(solution)/shard_map/ppermute | solution.py:18
  9.3 0.0 collective-permute-start.2
  9.3 2.4 %collective-permute-done.refs_1_ = bf16[2,8,16,256]{3,2,1,0:T(8,128)(2,1)S(1)} collective-permute-done((bf16[2,8,16,256]{3,2,1,0:T(8,128)(2,1)S(1)}, bf16[2,8,16,256]{3,2,1,0:T(8,128)(2,1)S(1)}, u32[]{:S(2)}, u32[]{:S(2)}) %collective-permute-start) | collective-permute-done | bytes 131104 | tf_op jit(solution)/shard_map/ppermute | solution.py:18
  11.7 7.9 %collective-permute-done.1.refs_2_ = bf16[2,8,16,256]{3,2,1,0:T(8,128)(2,1)S(1)} collective-permute-done((bf16[2,8,16,256]{3,2,1,0:T(8,128)(2,1)S(1)}, bf16[2,8,16,256]{3,2,1,0:T(8,128)(2,1)S(1)}, u32[]{:S(2)}, u32[]{:S(2)}) %collective-permute-start.1) | collective-permute-done | bytes 131104 | tf_op jit(solution)/shard_map/ppermute | solution.py:18
  19.6 0.0 collective-permute-done.2.refs_3_
  19.6 1.0 %cross.1 = (f32[2,32,256]{2,1,0:T(8,128)S(1)}, f32[2,32,256]{2,1,0:T(8,128)S(1)}, f32[2,32,256]{2,1,0:T(8,128)S(1)}, f32[2,32,256]{2,1,0:T(8,128)S(1)}) custom-call(s32[2,8]{1,0:T(2,128)S(1)} %bitcast.2, bf16[2,8,16,256]{3,2,1,0:T(8,128)(2,1)S(1)} %get-tuple-element.17.refs_0_, bf16[2,8,16,256]{3,2,1,0:T(8,128)(2,1)S(1)} %collective-permute-done.refs_1_, ...), custom_call_target="tpu_custom_call" | custom-call | tf_op jit(solution)/shard_map/cross/pallas_call | solution.py:189
  20.6 0.1 collective-permute-start.3
  20.7 1.6 %collective-permute-start.4 = (f32[2,32,256]{2,1,0:T(8,128)S(1)}, f32[2,32,256]{2,1,0:T(8,128)S(1)}, u32[]{:S(2)}, u32[]{:S(2)}) collective-permute-start(f32[2,32,256]{2,1,0:T(8,128)S(1)} %get-tuple-element.23), channel_id=1, source_target_pairs={{0,2},{1,3},{2,0},{3,1},{4,6},{5,7},{6,4},{7,5},{8,10},{9,11},{10,... | collective-permute-start | bytes 196616 | tf_op jit(solution)/shard_map/ppermute | solution.py:18
  22.2 0.3 %collective-permute-start.5 = (f32[2,32,256]{2,1,0:T(8,128)S(1)}, f32[2,32,256]{2,1,0:T(8,128)S(1)}, u32[]{:S(2)}, u32[]{:S(2)}) collective-permute-start(f32[2,32,256]{2,1,0:T(8,128)S(1)} %get-tuple-element.24), channel_id=1, source_target_pairs={{0,3},{1,2},{2,1},{3,0},{4,7},{5,6},{6,5},{7,4},{8,11},{9,10},{10,... | collective-permute-start | bytes 196616 | tf_op jit(solution)/shard_map/ppermute | solution.py:18
  22.5 5.1 %band_table.1 = (bf16[2,512,1024]{2,1,0:T(8,128)(2,1)S(1)}, bf16[2,512,1024]{2,1,0:T(8,128)(2,1)S(1)}) custom-call(), custom_call_target="tpu_custom_call" | custom-call | flops 20000000 | bytes 4000000 | tf_op jit(solution)/shard_map/band_table/pallas_call | solution.py:180
  27.6 0.0 collective-permute-done.3.refs_1_
  27.6 0.0 collective-permute-done.4.refs_2_
  27.6 0.0 collective-permute-done.5.refs_3_
  27.6 1.5 %lags.1 = f32[32,1024]{1,0:T(8,128)} custom-call(bf16[2,512,1024]{2,1,0:T(8,128)(2,1)S(1)} %get-tuple-element.15.high_ref, bf16[2,512,1024]{2,1,0:T(8,128)(2,1)S(1)} %get-tuple-element.16.low_ref, f32[2,32,256]{2,1,0:T(8,128)S(1)} %get-tuple-element.21.refs_0_, f32[2,32,256]{2,1,0:T(8,128)S(1)} %collective-permute-done.3.refs_1_, ...), custom_call_target="tpu_custom_call" | custom-call | tf_op jit(solution)/shard_map/lags/pallas_call | solution.py:203
Async XLA Ops:
  0.0 1.2 %copy-start = (bf16[8,128,2,256]{3,2,1,0:T(2,128)(2,1)S(1)}, bf16[8,128,2,256]{3,2,1,0:T(2,128)(2,1)}, u32[]{:S(2)}) copy-start(bf16[8,128,2,256]{3,2,1,0:T(2,128)(2,1)} %spectra_ref.1) | copy-start | bytes 3145732
  1.2 0.7 %copy-start.1 = (s32[8,128]{1,0:T(8,128)S(1)}, s32[8,128]{1,0:T(8,128)}, u32[]{:S(2)}) copy-start(s32[8,128]{1,0:T(8,128)} %uptime_ref.1) | copy-start | bytes 12292
  1.9 0.7 %copy-start.2 = (s32[8,2]{0,1:T(2,128)S(1)}, s32[8,2]{0,1:T(2,128)}, u32[]{:S(2)}) copy-start(s32[8,2]{0,1:T(2,128)} %param.5) | copy-start | bytes 196
  3.6 8.1 %collective-permute-start = (bf16[2,8,16,256]{3,2,1,0:T(8,128)(2,1)S(1)}, bf16[2,8,16,256]{3,2,1,0:T(8,128)(2,1)S(1)}, u32[]{:S(2)}, u32[]{:S(2)}) collective-permute-start(bf16[2,8,16,256]{3,2,1,0:T(8,128)(2,1)S(1)} %get-tuple-element.18), channel_id=1, source_target_pairs={{0,4},{4,0},{8,12},{12,8},{1,5},{5,1},{9,13},{13,9},{2,6},{6,2},{1... | collective-permute-start | bytes 393224 | tf_op jit(solution)/shard_map/ppermute | solution.py:18
  6.7 12.9 %collective-permute-start.1 = (bf16[2,8,16,256]{3,2,1,0:T(8,128)(2,1)S(1)}, bf16[2,8,16,256]{3,2,1,0:T(8,128)(2,1)S(1)}, u32[]{:S(2)}, u32[]{:S(2)}) collective-permute-start(bf16[2,8,16,256]{3,2,1,0:T(8,128)(2,1)S(1)} %get-tuple-element.19), channel_id=1, source_target_pairs={{0,8},{4,12},{8,0},{12,4},{1,9},{5,13},{9,1},{13,5},{2,10},{6,14},... | collective-permute-start | bytes 393224 | tf_op jit(solution)/shard_map/ppermute | solution.py:18
  9.3 10.3 %collective-permute-start.2 = (bf16[2,8,16,256]{3,2,1,0:T(8,128)(2,1)S(1)}, bf16[2,8,16,256]{3,2,1,0:T(8,128)(2,1)S(1)}, u32[]{:S(2)}, u32[]{:S(2)}) collective-permute-start(bf16[2,8,16,256]{3,2,1,0:T(8,128)(2,1)S(1)} %get-tuple-element.20), channel_id=1, source_target_pairs={{0,12},{4,8},{8,4},{12,0},{1,13},{5,9},{9,5},{13,1},{2,14},{6,10},... | collective-permute-start | bytes 393224 | tf_op jit(solution)/shard_map/ppermute | solution.py:18
  20.6 7.0 %collective-permute-start.3 = (f32[2,32,256]{2,1,0:T(8,128)S(1)}, f32[2,32,256]{2,1,0:T(8,128)S(1)}, u32[]{:S(2)}, u32[]{:S(2)}) collective-permute-start(f32[2,32,256]{2,1,0:T(8,128)S(1)} %get-tuple-element.22), channel_id=1, source_target_pairs={{0,1},{1,0},{2,3},{3,2},{4,5},{5,4},{6,7},{7,6},{8,9},{9,8},{10,11... | collective-permute-start | bytes 196616 | tf_op jit(solution)/shard_map/ppermute | solution.py:18
  20.7 7.0 %collective-permute-start.4 = (f32[2,32,256]{2,1,0:T(8,128)S(1)}, f32[2,32,256]{2,1,0:T(8,128)S(1)}, u32[]{:S(2)}, u32[]{:S(2)}) collective-permute-start(f32[2,32,256]{2,1,0:T(8,128)S(1)} %get-tuple-element.23), channel_id=1, source_target_pairs={{0,2},{1,3},{2,0},{3,1},{4,6},{5,7},{6,4},{7,5},{8,10},{9,11},{10,... | collective-permute-start | bytes 196616 | tf_op jit(solution)/shard_map/ppermute | solution.py:18
  22.2 5.4 %collective-permute-start.5 = (f32[2,32,256]{2,1,0:T(8,128)S(1)}, f32[2,32,256]{2,1,0:T(8,128)S(1)}, u32[]{:S(2)}, u32[]{:S(2)}) collective-permute-start(f32[2,32,256]{2,1,0:T(8,128)S(1)} %get-tuple-element.24), channel_id=1, source_target_pairs={{0,3},{1,2},{2,1},{3,0},{4,7},{5,6},{6,5},{7,4},{8,11},{9,10},{10,... | collective-permute-start | bytes 196616 | tf_op jit(solution)/shard_map/ppermute | solution.py:18

commit v2 on v1

--- a/solution.py
+++ b/solution.py
@@ -18,13 +18,26 @@
     return lax.ppermute(x, axes, [(i, i ^ distance) for i in range(size)])
 
 
-def slots_kernel(readers, pairs_ref, uptime_ref, spectra_ref, *out_refs):
+def slots_kernel(readers, pairs_hbm, uptime_hbm, spectra_hbm, *refs):
+    out_refs, (pairs_out, pairs_ref, uptime_ref, spectra_ref, sems) = refs[:readers], refs[readers:]
     me = lax.axis_index("stn")
     hours, stations = uptime_ref.shape
     freq_loc = spectra_ref.shape[3]
     owned = stations // SB
     reader_blocks = pairs_ref.shape[1] // readers
     rows = SB * 2
+    copies = [
+        pltpu.make_async_copy(pairs_hbm, pairs_ref, sems.at[0]),
+        pltpu.make_async_copy(uptime_hbm, uptime_ref, sems.at[1]),
+        pltpu.make_async_copy(pairs_hbm, pairs_out, sems.at[2]),
+    ] + [
+        pltpu.make_async_copy(spectra_hbm.at[h], spectra_ref.at[h], sems.at[3 + h])
+        for h in range(hours)
+    ]
+    for copy in copies:
+        copy.start()
+    for copy in copies:
+        copy.wait()
     up = uptime_ref[...].astype(jnp.float32).astype(jnp.bfloat16)
     for distance in range(readers):
         reader = me ^ distance
@@ -51,26 +64,32 @@
                 out_refs[distance][slot, hour] = jnp.where(keep, values, 0.0).astype(jnp.bfloat16)
 
 
-def cross_kernel(readers, parts, freq_parts, owned, pairs_ref, *refs):
+def cross_kernel(order, parts, freq_parts, owned, pairs_ref, table_ref, *refs):
+    del table_ref
+    readers = len(order)
     slot_refs, out_refs, blocks = refs[:readers], refs[readers : readers + parts], refs[-1]
     me = lax.axis_index("stn")
     mine = lax.axis_index("hour") * freq_parts + lax.axis_index("freq")
     reader_blocks = pairs_ref.shape[1] // readers
     _, chunks, hours, _, _ = blocks.shape
-    wanted = [
-        pairs_ref[entry % 2, me * reader_blocks + entry // 2] for entry in range(2 * reader_blocks)
-    ]
+    pairs = pairs_ref[...]
+    side = lax.broadcasted_iota(jnp.int32, pairs.shape, 0)
+    column = lax.broadcasted_iota(jnp.int32, pairs.shape, 1)
+    wanted = []
+    for entry in range(2 * reader_blocks):
+        here = (side == entry % 2) & (column == me * reader_blocks + entry // 2)
+        wanted.append(jnp.max(jnp.where(here, pairs, 0)))
     owners = [block // owned for block in wanted]
     for entry in range(2 * reader_blocks):
         slot = jnp.int32(0)
         for before in range(entry):
             slot = slot + (owners[before] == owners[entry]).astype(jnp.int32)
         slot = jnp.minimum(slot, CAP - 1)
-        for distance in range(readers):
+        for slot_ref, distance in zip(slot_refs, order, strict=True):
 
             @pl.when(owners[entry] == me ^ distance)
-            def _(entry=entry, slot=slot, distance=distance):
-                values = slot_refs[distance][slot].astype(jnp.float32)
+            def _(entry=entry, slot=slot, slot_ref=slot_ref):
+                values = slot_ref[slot].astype(jnp.float32)
                 for chunk in range(blocks.shape[1]):
                     blocks[entry, chunk] = values[:, :, chunk * LANES : (chunk + 1) * LANES]
 
@@ -160,22 +179,28 @@
     part_pairs = reader_blocks * SB * SB // parts
     pairs = pair_blocks.T
     vmem = pl.BlockSpec(memory_space=pltpu.VMEM)
-    smem = pl.BlockSpec(memory_space=pltpu.SMEM)
+    whole = pl.BlockSpec(memory_space=pl.ANY)
+    hbm = pl.BlockSpec(memory_space=pltpu.HBM)
     limit = pltpu.CompilerParams(vmem_limit_bytes=32 * 1024 * 1024)
 
-    slots = pl.pallas_call(
+    *slots, wanted = pl.pallas_call(
         functools.partial(slots_kernel, readers),
-        out_shape=[jax.ShapeDtypeStruct((CAP, hours, 2 * SB, freq_loc), jnp.bfloat16)] * readers,
-        in_specs=[smem, vmem, vmem],
-        out_specs=[vmem] * readers,
+        out_shape=[jax.ShapeDtypeStruct((CAP, hours, 2 * SB, freq_loc), jnp.bfloat16)] * readers
+        + [jax.ShapeDtypeStruct(pairs.shape, jnp.int32)],
+        in_specs=[hbm] * 3,
+        out_specs=[vmem] * (readers + 1),
+        scratch_shapes=[
+            pltpu.SMEM(pairs.shape, jnp.int32),
+            pltpu.VMEM(uptime.shape, jnp.int32),
+            pltpu.VMEM(spectra.shape, jnp.bfloat16),
+            pltpu.SemaphoreType.DMA((3 + hours,)),
+        ],
         compiler_params=limit,
         name="slots",
     )(pairs, uptime, spectra)
 
     order = sorted(range(1, readers), key=lambda d: (d < readers // 2, d))
-    arrived = [slots[0]] + [None] * (readers - 1)
-    for distance in order:
-        arrived[distance] = exchange(slots[distance], "stn", readers, distance)
+    arrived = [exchange(slots[distance], "stn", readers, distance) for distance in order]
 
     high, low = pl.pallas_call(
         functools.partial(table_kernel, hours * hour_parts),
@@ -187,14 +212,14 @@
     )()
 
     cross = pl.pallas_call(
-        functools.partial(cross_kernel, readers, parts, freq_parts, stations // SB),
+        functools.partial(cross_kernel, order + [0], parts, freq_parts, stations // SB),
         out_shape=[jax.ShapeDtypeStruct((2, part_pairs, freq_loc), jnp.float32)] * parts,
-        in_specs=[smem] + [vmem] * readers,
+        in_specs=[vmem, whole] + [vmem] * readers,
         out_specs=[vmem] * parts,
         scratch_shapes=[pltpu.VMEM((2 * reader_blocks, freq_loc // LANES, hours, 2 * SB, LANES), jnp.float32)],
         compiler_params=limit,
         name="cross",
-    )(pairs, *arrived)
+    )(wanted, high, *arrived, slots[0])
 
     summed = [cross[0]] + [
         exchange(cross[distance], ("hour", "freq"), parts, distance) for distance in range(1, parts)

time: 29.3 us -> 27.5 us (0.939)
  the two profiles are of different devices: /device:TPU:0 before, /device:TPU:21 now
where the time goes in v2:
time: 27.5 us; the launch traced here: 27.3 us
  waiting for transfers between devices  9.71 us (35%)
  Pallas kernels  9.07 us (33%)
  starting transfers between devices  5.88 us (21%)
  local copies, waits for them, and re-layouts  2.59 us (9%)
    ppermute x6, waiting for transfers between devices, exchange(): return lax.ppermute(x, axes, [(i, i ^ distance) for i in range(size)])  9.71 us
    ppermute x6, starting transfers between devices, exchange(): return lax.ppermute(x, axes, [(i, i ^ distance) for i in range(size)])  5.88 us
    pallas_call x1, Pallas kernels, per_device(): pl.pallas_call(functools.partial(table_kernel, hours * hour_parts), out_s...  5.08 us
    unnamed x6, local copies, waits for them, and re-layouts  2.59 us
    pallas_call x1, Pallas kernels, per_device(): pl.pallas_call(functools.partial(slots_kernel, readers), out_shape=[jax.S...  1.89 us
    pallas_call x1, Pallas kernels, per_device(): pl.pallas_call(functools.partial(lags_kernel, parts, freq_parts), out_sha...  1.49 us
    pallas_call x1, Pallas kernels, per_device(): pl.pallas_call(functools.partial(cross_kernel, order + [0], parts, freq_p...  0.61 us
  transfers between devices with their start and end apart: 6, of which 3 were waited for; matrix products, arithmetic and copies ran while one was open for 0% of the time, Pallas kernels for 19%

profile of v2, /device:TPU:21, one launch (start us, length us, event | category | flops | bytes accessed | tf_op | source)
XLA Modules:
  0.0 27.3 jit_solution(13838901426752630875)
XLA Ops:
  0.0 0.0 copy-start
  0.0 1.2 %copy-done = bf16[8,128,2,256]{3,2,1,0:T(2,128)(2,1)S(1)} copy-done((bf16[8,128,2,256]{3,2,1,0:T(2,128)(2,1)S(1)}, bf16[8,128,2,256]{3,2,1,0:T(2,128)(2,1)}, u32[]{:S(2)}) %copy-start) | copy-done | bytes 1048600
  1.2 0.0 copy-start.1
  1.2 0.7 %copy-done.1 = s32[8,128]{1,0:T(8,128)S(1)} copy-done((s32[8,128]{1,0:T(8,128)S(1)}, s32[8,128]{1,0:T(8,128)}, u32[]{:S(2)}) %copy-start.1) | copy-done | bytes 4120
  1.9 0.0 copy-start.2
  1.9 0.7 %copy-done.2 = s32[8,2]{0,1:T(2,128)S(1)} copy-done((s32[8,2]{0,1:T(2,128)S(1)}, s32[8,2]{0,1:T(2,128)}, u32[]{:S(2)}) %copy-start.2) | copy-done | bytes 88
  2.6 1.9 %slots.1 = (bf16[2,8,16,256]{3,2,1,0:T(8,128)(2,1)S(1)}, bf16[2,8,16,256]{3,2,1,0:T(8,128)(2,1)S(1)}, bf16[2,8,16,256]{3,2,1,0:T(8,128)(2,1)S(1)}, bf16[2,8,16,256]{3,2,1,0:T(8,128)(2,1)S(1)}, s32[2,8]{1,0:T(2,128)S(1)}) custom-call(s32[2,8]{1,0:T(2,128)S(1)} %bitcast.1, s32[8,128]{1,0:T(8,128)S(1)} %copy-done.1, bf16[8,128,2,256]{3,2,1,0:T(2,128)(2,1)S(1)} %copy-done), custom_call_target="tpu_custom_call" | custom-call | tf_op jit(solution)/shard_map/slots/pallas_call | solution.py:186
  4.5 0.1 collective-permute-start
  4.6 2.4 %collective-permute-start.1 = (bf16[2,8,16,256]{3,2,1,0:T(8,128)(2,1)S(1)}, bf16[2,8,16,256]{3,2,1,0:T(8,128)(2,1)S(1)}, u32[]{:S(2)}, u32[]{:S(2)}) collective-permute-start(bf16[2,8,16,256]{3,2,1,0:T(8,128)(2,1)S(1)} %get-tuple-element.20), channel_id=1, source_target_pairs={{0,12},{4,8},{8,4},{12,0},{1,13},{5,9},{9,5},{13,1},{2,14},{6,10},... | collective-permute-start | bytes 393224 | tf_op jit(solution)/shard_map/ppermute | solution.py:18
  7.0 1.1 %collective-permute-start.2 = (bf16[2,8,16,256]{3,2,1,0:T(8,128)(2,1)S(1)}, bf16[2,8,16,256]{3,2,1,0:T(8,128)(2,1)S(1)}, u32[]{:S(2)}, u32[]{:S(2)}) collective-permute-start(bf16[2,8,16,256]{3,2,1,0:T(8,128)(2,1)S(1)} %get-tuple-element.21), channel_id=1, source_target_pairs={{0,4},{4,0},{8,12},{12,8},{1,5},{5,1},{9,13},{13,9},{2,6},{6,2},{1... | collective-permute-start | bytes 393224 | tf_op jit(solution)/shard_map/ppermute | solution.py:18
  8.1 5.1 %band_table.1 = (bf16[2,512,1024]{2,1,0:T(8,128)(2,1)S(1)}, bf16[2,512,1024]{2,1,0:T(8,128)(2,1)S(1)}) custom-call(), custom_call_target="tpu_custom_call" | custom-call | flops 20000000 | bytes 4000000 | tf_op jit(solution)/shard_map/band_table/pallas_call | solution.py:205
  13.2 0.0 collective-permute-done.refs_0_
  13.2 6.1 %collective-permute-done.1.refs_1_ = bf16[2,8,16,256]{3,2,1,0:T(8,128)(2,1)S(1)} collective-permute-done((bf16[2,8,16,256]{3,2,1,0:T(8,128)(2,1)S(1)}, bf16[2,8,16,256]{3,2,1,0:T(8,128)(2,1)S(1)}, u32[]{:S(2)}, u32[]{:S(2)}) %collective-permute-start.1) | collective-permute-done | bytes 131104 | tf_op jit(solution)/shard_map/ppermute | solution.py:18
  19.3 0.0 collective-permute-done.2.refs_2_
  19.3 0.6 %cross.1 = (f32[2,32,256]{2,1,0:T(8,128)S(1)}, f32[2,32,256]{2,1,0:T(8,128)S(1)}, f32[2,32,256]{2,1,0:T(8,128)S(1)}, f32[2,32,256]{2,1,0:T(8,128)S(1)}) custom-call(s32[2,8]{1,0:T(2,128)S(1)} %get-tuple-element.18.pairs_ref, bf16[2,512,1024]{2,1,0:T(8,128)(2,1)S(1)} %get-tuple-element.16.table_ref.high_ref, ...), custom_call_target="tpu_custom_call" | custom-call | tf_op jit(solution)/shard_map/cross/pallas_call | solution.py:214
  20.0 0.6 %collective-permute-start.3 = (f32[2,32,256]{2,1,0:T(8,128)S(1)}, f32[2,32,256]{2,1,0:T(8,128)S(1)}, u32[]{:S(2)}, u32[]{:S(2)}) collective-permute-start(f32[2,32,256]{2,1,0:T(8,128)S(1)} %get-tuple-element.24), channel_id=1, source_target_pairs={{0,1},{1,0},{2,3},{3,2},{4,5},{5,4},{6,7},{7,6},{8,9},{9,8},{10,11... | collective-permute-start | bytes 196616 | tf_op jit(solution)/shard_map/ppermute | solution.py:18
  20.5 1.2 %collective-permute-start.4 = (f32[2,32,256]{2,1,0:T(8,128)S(1)}, f32[2,32,256]{2,1,0:T(8,128)S(1)}, u32[]{:S(2)}, u32[]{:S(2)}) collective-permute-start(f32[2,32,256]{2,1,0:T(8,128)S(1)} %get-tuple-element.25), channel_id=1, source_target_pairs={{0,2},{1,3},{2,0},{3,1},{4,6},{5,7},{6,4},{7,5},{8,10},{9,11},{10,... | collective-permute-start | bytes 196616 | tf_op jit(solution)/shard_map/ppermute | solution.py:18
  21.7 0.5 %collective-permute-start.5 = (f32[2,32,256]{2,1,0:T(8,128)S(1)}, f32[2,32,256]{2,1,0:T(8,128)S(1)}, u32[]{:S(2)}, u32[]{:S(2)}) collective-permute-start(f32[2,32,256]{2,1,0:T(8,128)S(1)} %get-tuple-element.26), channel_id=1, source_target_pairs={{0,3},{1,2},{2,1},{3,0},{4,7},{5,6},{6,5},{7,4},{8,11},{9,10},{10,... | collective-permute-start | bytes 196616 | tf_op jit(solution)/shard_map/ppermute | solution.py:18
  22.2 0.0 collective-permute-done.3.refs_1_
  22.2 2.0 %collective-permute-done.4.refs_2_ = f32[2,32,256]{2,1,0:T(8,128)S(1)} collective-permute-done((f32[2,32,256]{2,1,0:T(8,128)S(1)}, f32[2,32,256]{2,1,0:T(8,128)S(1)}, u32[]{:S(2)}, u32[]{:S(2)}) %collective-permute-start.4) | collective-permute-done | bytes 65568 | tf_op jit(solution)/shard_map/ppermute | solution.py:18
  24.2 1.6 %collective-permute-done.5.refs_3_ = f32[2,32,256]{2,1,0:T(8,128)S(1)} collective-permute-done((f32[2,32,256]{2,1,0:T(8,128)S(1)}, f32[2,32,256]{2,1,0:T(8,128)S(1)}, u32[]{:S(2)}, u32[]{:S(2)}) %collective-permute-start.5) | collective-permute-done | bytes 65568 | tf_op jit(solution)/shard_map/ppermute | solution.py:18
  25.8 1.5 %lags.1 = f32[32,1024]{1,0:T(8,128)} custom-call(bf16[2,512,1024]{2,1,0:T(8,128)(2,1)S(1)} %get-tuple-element.16.table_ref.high_ref, bf16[2,512,1024]{2,1,0:T(8,128)(2,1)S(1)} %get-tuple-element.17.low_ref, f32[2,32,256]{2,1,0:T(8,128)S(1)} %get-tuple-element.23.refs_0_, f32[2,32,256]{2,1,0:T(8,128)S(1)} %collective-permute-done.3.refs_1_, ...), custom_call_target="tpu_custom_call" | custom-call | tf_op jit(solution)/shard_map/lags/pallas_call | solution.py:228
Async XLA Ops:
  0.0 1.2 %copy-start = (bf16[8,128,2,256]{3,2,1,0:T(2,128)(2,1)S(1)}, bf16[8,128,2,256]{3,2,1,0:T(2,128)(2,1)}, u32[]{:S(2)}) copy-start(bf16[8,128,2,256]{3,2,1,0:T(2,128)(2,1)} %spectra_hbm.1) | copy-start | bytes 3145732
  1.2 0.7 %copy-start.1 = (s32[8,128]{1,0:T(8,128)S(1)}, s32[8,128]{1,0:T(8,128)}, u32[]{:S(2)}) copy-start(s32[8,128]{1,0:T(8,128)} %uptime_hbm.1) | copy-start | bytes 12292
  1.9 0.7 %copy-start.2 = (s32[8,2]{0,1:T(2,128)S(1)}, s32[8,2]{0,1:T(2,128)}, u32[]{:S(2)}) copy-start(s32[8,2]{0,1:T(2,128)} %param.5) | copy-start | bytes 196
  4.5 8.7 %collective-permute-start = (bf16[2,8,16,256]{3,2,1,0:T(8,128)(2,1)S(1)}, bf16[2,8,16,256]{3,2,1,0:T(8,128)(2,1)S(1)}, u32[]{:S(2)}, u32[]{:S(2)}) collective-permute-start(bf16[2,8,16,256]{3,2,1,0:T(8,128)(2,1)S(1)} %get-tuple-element.19), channel_id=1, source_target_pairs={{0,8},{4,12},{8,0},{12,4},{1,9},{5,13},{9,1},{13,5},{2,10},{6,14},... | collective-permute-start | bytes 393224 | tf_op jit(solution)/shard_map/ppermute | solution.py:18
  4.6 14.7 %collective-permute-start.1 = (bf16[2,8,16,256]{3,2,1,0:T(8,128)(2,1)S(1)}, bf16[2,8,16,256]{3,2,1,0:T(8,128)(2,1)S(1)}, u32[]{:S(2)}, u32[]{:S(2)}) collective-permute-start(bf16[2,8,16,256]{3,2,1,0:T(8,128)(2,1)S(1)} %get-tuple-element.20), channel_id=1, source_target_pairs={{0,12},{4,8},{8,4},{12,0},{1,13},{5,9},{9,5},{13,1},{2,14},{6,10},... | collective-permute-start | bytes 393224 | tf_op jit(solution)/shard_map/ppermute | solution.py:18
  7.0 12.3 %collective-permute-start.2 = (bf16[2,8,16,256]{3,2,1,0:T(8,128)(2,1)S(1)}, bf16[2,8,16,256]{3,2,1,0:T(8,128)(2,1)S(1)}, u32[]{:S(2)}, u32[]{:S(2)}) collective-permute-start(bf16[2,8,16,256]{3,2,1,0:T(8,128)(2,1)S(1)} %get-tuple-element.21), channel_id=1, source_target_pairs={{0,4},{4,0},{8,12},{12,8},{1,5},{5,1},{9,13},{13,9},{2,6},{6,2},{1... | collective-permute-start | bytes 393224 | tf_op jit(solution)/shard_map/ppermute | solution.py:18
  20.0 2.3 %collective-permute-start.3 = (f32[2,32,256]{2,1,0:T(8,128)S(1)}, f32[2,32,256]{2,1,0:T(8,128)S(1)}, u32[]{:S(2)}, u32[]{:S(2)}) collective-permute-start(f32[2,32,256]{2,1,0:T(8,128)S(1)} %get-tuple-element.24), channel_id=1, source_target_pairs={{0,1},{1,0},{2,3},{3,2},{4,5},{5,4},{6,7},{7,6},{8,9},{9,8},{10,11... | collective-permute-start | bytes 196616 | tf_op jit(solution)/shard_map/ppermute | solution.py:18
  20.5 3.7 %collective-permute-start.4 = (f32[2,32,256]{2,1,0:T(8,128)S(1)}, f32[2,32,256]{2,1,0:T(8,128)S(1)}, u32[]{:S(2)}, u32[]{:S(2)}) collective-permute-start(f32[2,32,256]{2,1,0:T(8,128)S(1)} %get-tuple-element.25), channel_id=1, source_target_pairs={{0,2},{1,3},{2,0},{3,1},{4,6},{5,7},{6,4},{7,5},{8,10},{9,11},{10,... | collective-permute-start | bytes 196616 | tf_op jit(solution)/shard_map/ppermute | solution.py:18
  21.7 4.0 %collective-permute-start.5 = (f32[2,32,256]{2,1,0:T(8,128)S(1)}, f32[2,32,256]{2,1,0:T(8,128)S(1)}, u32[]{:S(2)}, u32[]{:S(2)}) collective-permute-start(f32[2,32,256]{2,1,0:T(8,128)S(1)} %get-tuple-element.26), channel_id=1, source_target_pairs={{0,3},{1,2},{2,1},{3,0},{4,7},{5,6},{6,5},{7,4},{8,11},{9,10},{10,... | collective-permute-start | bytes 196616 | tf_op jit(solution)/shard_map/ppermute | solution.py:18

commit v3 on v2

v3 whole, which is shorter than its diff:
```python
import functools
import math

import jax
import jax.numpy as jnp
from jax import lax
from jax.experimental import pallas as pl
from jax.experimental.pallas import tpu as pltpu
from jax.sharding import PartitionSpec as P

L = 1024
SB = 8
CAP = 2
LANES = 128
QUARTER = L // 4


def exchange(x, axes, size, distance):
    return lax.ppermute(x, axes, [(i, i ^ distance) for i in range(size)])


def wanted_slots(pairs_ref, reader, me, reader_blocks, owned):
    starts = [jnp.int32(0)] * CAP
    found = jnp.int32(0)
    for entry in range(2 * reader_blocks):
        block = pairs_ref[entry % 2, reader * reader_blocks + entry // 2]
        mine = (block >= me * owned) & (block < (me + 1) * owned)
        for slot in range(CAP):
            starts[slot] = jnp.where(mine & (found == slot), (block - me * owned) * SB, starts[slot])
        found = found + mine.astype(jnp.int32)
    return starts


def recorded_rows(start, up):
    rows = 2 * SB
    station = lax.broadcasted_iota(jnp.int32, (rows, up.shape[1]), 1)
    row = lax.broadcasted_iota(jnp.int32, (rows, up.shape[1]), 0)
    pick = (station == start + row // 2).astype(jnp.float32).astype(jnp.bfloat16)
    return lax.dot_general(
        pick, up, (((1,), (1,)), ((), ())), preferred_element_type=jnp.float32
    )


def masked_rows(spectra_ref, hour, start, recorded):
    values = spectra_ref[hour, pl.ds(start, SB)].astype(jnp.float32)
    values = values.reshape(2 * SB, spectra_ref.shape[3])
    keep = jnp.broadcast_to(recorded[:, hour : hour + 1], values.shape) > 0
    return jnp.where(keep, values, 0.0).astype(jnp.bfloat16)


def write_slots(pairs_ref, up, spectra_ref, readers, distances, hours_ready, out_refs):
    me = lax.axis_index("stn")
    stations = up.shape[1]
    reader_blocks = pairs_ref.shape[1] // readers
    wanted = []
    for out_ref, distance in zip(out_refs, distances, strict=True):
        starts = wanted_slots(pairs_ref, me ^ distance, me, reader_blocks, stations // SB)
        for slot, start in enumerate(starts):
            wanted.append((out_ref, slot, start, recorded_rows(start, up)))
    for hour in range(spectra_ref.shape[0]):
        if hours_ready is not None:
            hours_ready[hour].wait()
        for out_ref, slot, start, recorded in wanted:
            out_ref[slot, hour] = masked_rows(spectra_ref, hour, start, recorded)


def send_kernel(readers, distances, pairs_hbm, uptime_hbm, spectra_hbm, *refs):
    out_refs, (pairs_out, pairs_ref, uptime_ref, spectra_ref, sems) = refs[:-5], refs[-5:]
    arguments = [
        pltpu.make_async_copy(pairs_hbm, pairs_ref, sems.at[0]),
        pltpu.make_async_copy(uptime_hbm, uptime_ref, sems.at[1]),
        pltpu.make_async_copy(pairs_hbm, pairs_out, sems.at[2]),
    ]
    spectra = [
        pltpu.make_async_copy(spectra_hbm.at[h], spectra_ref.at[h], sems.at[3 + h])
        for h in range(spectra_ref.shape[0])
    ]
    for copy in arguments + spectra:
        copy.start()
    for copy in arguments:
        copy.wait()
    up = uptime_ref[...].astype(jnp.float32).astype(jnp.bfloat16)
    write_slots(pairs_ref, up, spectra_ref, readers, distances, spectra, out_refs)


def prepare_kernel(readers, hour_total, pairs_ref, uptime_ref, spectra_ref, *refs):
    high_ref, low_ref, own_ref = refs
    up = uptime_ref[...].astype(jnp.float32).astype(jnp.bfloat16)
    write_slots(pairs_ref, up, spectra_ref, readers, [0], None, [own_ref])

    _, chunks, _, lags = high_ref.shape
    half = L // 2
    tall = 16
    groups = half // tall
    sub = lax.broadcasted_iota(jnp.int32, (tall, LANES), 0)
    lane = lax.broadcasted_iota(jnp.int32, (tall, LANES), 1)
    base_cos, base_sin = circle(sub * lane, L)
    group_cos, group_sin = circle(
        lax.broadcasted_iota(jnp.int32, (groups, LANES), 0)
        * lax.broadcasted_iota(jnp.int32, (groups, LANES), 1),
        L // tall,
    )
    steps = [circle(sub * j, L // LANES) for j in range(1, lags // LANES)]
    weight_cos, weight_sin = circle(2 * sub + 1, 2 * L)
    scale = 1.0 / math.sqrt(hour_total * half)
    for group in range(groups):
        turn_cos, turn_sin = group_cos[group : group + 1], group_sin[group : group + 1]
        quarter_turns = math.pi * tall * group / half
        weight = weight_sin * math.cos(quarter_turns) + weight_cos * math.sin(quarter_turns)
        weight = weight * weight * scale
        cos0 = (base_cos * turn_cos - base_sin * turn_sin) * weight
        sin0 = (base_sin * turn_cos + base_cos * turn_sin) * weight
        row = group % (LANES // tall) * tall
        at = group // (LANES // tall)
        for j in range(lags // LANES):
            real, imag = cos0, -sin0
            if j > 0:
                cj, sj = steps[j - 1]
                real, imag = cos0 * cj - sin0 * sj, -(sin0 * cj + cos0 * sj)
            for first, value in ((row, real), (LANES + row, imag)):
                where = (at // chunks, at % chunks, pl.ds(first, tall), pl.ds(j * LANES, LANES))
                high = value.astype(jnp.bfloat16)
                high_ref[where] = high
                low_ref[where] = (value - high.astype(jnp.float32)).astype(jnp.bfloat16)


def circle(step, steps):
    quarter = steps // 4
    step = step % steps
    turn = (step + quarter // 2) // quarter
    x = (step - turn * quarter).astype(jnp.float32) * (2.0 * math.pi / steps)
    y = x * x
    sin = x * (1.0 + y * (-1 / 6 + y * (1 / 120 + y * (-1 / 5040 + y * (1 / 362880)))))
    cos = 1.0 + y * (-1 / 2 + y * (1 / 24 + y * (-1 / 720 + y * (1 / 40320 - y * (1 / 3628800)))))
    turn = turn % 4
    odd = turn % 2 == 1
    out_cos, out_sin = jnp.where(odd, sin, cos), jnp.where(odd, cos, sin)
    out_cos = jnp.where((turn == 1) | (turn == 2), -out_cos, out_cos)
    out_sin = jnp.where((turn == 2) | (turn == 3), -out_sin, out_sin)
    return out_cos, out_sin


def cross_kernel(distances, parts, freq_parts, owned, pairs_ref, *refs):
    readers = len(distances)
    slot_refs, out_refs, blocks = refs[:readers], refs[readers : readers + parts], refs[-1]
    me = lax.axis_index("stn")
    mine = lax.axis_index("hour") * freq_parts + lax.axis_index("freq")
    reader_blocks = pairs_ref.shape[1] // readers
    _, chunks, hours, _, _ = blocks.shape
    pairs = pairs_ref[...]
    side = lax.broadcasted_iota(jnp.int32, pairs.shape, 0)
    column = lax.broadcasted_iota(jnp.int32, pairs.shape, 1)
    wanted = []
    for entry in range(2 * reader_blocks):
        here = (side == entry % 2) & (column == me * reader_blocks + entry // 2)
        wanted.append(jnp.max(jnp.where(here, pairs, 0)))
    owners = [block // owned for block in wanted]
    for entry in range(2 * reader_blocks):
        slot = jnp.int32(0)
        for before in range(entry):
            slot = slot + (owners[before] == owners[entry]).astype(jnp.int32)
        slot = jnp.minimum(slot, CAP - 1)
        for slot_ref, distance in zip(slot_refs, distances, strict=True):

            @pl.when(owners[entry] == me ^ distance)
            def _(entry=entry, slot=slot, slot_ref=slot_ref):
                values = slot_ref[slot].astype(jnp.float32)
                for chunk in range(chunks):
                    blocks[entry, chunk] = values[:, :, chunk * LANES : (chunk + 1) * LANES]

    part_rows = out_refs[0].shape[1] // SB
    for distance in range(parts):
        first_row = (mine ^ distance) * part_rows
        pair = first_row // SB
        station = first_row % SB
        for chunk in range(chunks):
            lanes = pl.ds(chunk * LANES, LANES)
            second = 2 * pair + 1
            second_re = [blocks[second, chunk, h, pl.ds(0, SB, stride=2)] for h in range(hours)]
            second_im = [blocks[second, chunk, h, pl.ds(1, SB, stride=2)] for h in range(hours)]
            for s in range(part_rows):
                real = jnp.zeros((SB, LANES), jnp.float32)
                imag = jnp.zeros((SB, LANES), jnp.float32)
                for h in range(hours):
                    first_re = blocks[2 * pair, chunk, h, pl.ds(2 * (station + s), 1)]
                    first_im = blocks[2 * pair, chunk, h, pl.ds(2 * (station + s) + 1, 1)]
                    real = real + first_re * second_re[h] + first_im * second_im[h]
                    imag = imag + first_im * second_re[h] - first_re * second_im[h]
                out_refs[distance][0, pl.ds(s * SB, SB), lanes] = real
                out_refs[distance][1, pl.ds(s * SB, SB), lanes] = imag


def lags_kernel(parts, freq_parts, high_ref, low_ref, *refs):
    part_refs, out_ref = refs[:-1], refs[-1]
    own = lax.axis_index("freq")
    count = out_ref.shape[0]
    phase = lax.broadcasted_iota(jnp.int32, (count, LANES), 1) % 4
    total = None
    for c in range(freq_parts):
        for chunk in range(high_ref.shape[1]):
            lanes = pl.ds(chunk * LANES, LANES)
            cross = part_refs[c][:, :, lanes]
            for x in range(1, parts // freq_parts):
                cross = cross + part_refs[x * freq_parts + c][:, :, lanes]
            real, imag = cross[0], cross[1]
            turned = []
            for q in range(4):
                step = (phase * q) % 4
                re = jnp.where(step % 2 == 0, real, imag)
                im = jnp.where(step % 2 == 0, imag, real)
                re = jnp.where((step == 1) | (step == 2), -re, re)
                im = jnp.where((step == 2) | (step == 3), -im, im)
                turned.append(jnp.concatenate([re, im], axis=1))
            turned = jnp.concatenate(turned, axis=0)
            high = turned.astype(jnp.bfloat16)
            low = (turned - high.astype(jnp.float32)).astype(jnp.bfloat16)
            table_high = high_ref[own ^ c, chunk]
            term = (
                jnp.dot(high, table_high, preferred_element_type=jnp.float32)
                + jnp.dot(low, table_high, preferred_element_type=jnp.float32)
                + jnp.dot(high, low_ref[own ^ c, chunk], preferred_element_type=jnp.float32)
            )
            total = term if total is None else total + term
    for q in range(4):
        out_ref[:, q * QUARTER : (q + 1) * QUARTER] = total[q * count : (q + 1) * count]


def per_device(sizes, spectra, uptime, pair_blocks):
    readers, hour_parts, freq_parts = sizes
    hours, stations, _, freq_loc = spectra.shape
    parts = hour_parts * freq_parts
    chunks = freq_loc // LANES
    reader_blocks = pair_blocks.shape[0] // readers
    part_pairs = reader_blocks * SB * SB // parts
    pairs = pair_blocks.T
    vmem = pl.BlockSpec(memory_space=pltpu.VMEM)
    smem = pl.BlockSpec(memory_space=pltpu.SMEM)
    hbm = pl.BlockSpec(memory_space=pltpu.HBM)
    limit = pltpu.CompilerParams(vmem_limit_bytes=32 * 1024 * 1024)
    slots_shape = jax.ShapeDtypeStruct((CAP, hours, 2 * SB, freq_loc), jnp.bfloat16)
    pairs_shape = jax.ShapeDtypeStruct(pairs.shape, jnp.int32)

    distances = [*range(readers // 2, readers), *range(1, readers // 2)]
    *sent, wanted = pl.pallas_call(
        functools.partial(send_kernel, readers, distances),
        out_shape=[slots_shape] * len(distances) + [pairs_shape],
        in_specs=[hbm] * 3,
        out_specs=[vmem] * (len(distances) + 1),
        scratch_shapes=[
            pltpu.SMEM(pairs.shape, jnp.int32),
            pltpu.VMEM(uptime.shape, jnp.int32),
            pltpu.VMEM(spectra.shape, jnp.bfloat16),
            pltpu.SemaphoreType.DMA((3 + hours,)),
        ],
        compiler_params=limit,
        name="send_slots",
    )(*[pltpu.with_memory_space_constraint(x, pltpu.HBM) for x in (pairs, uptime, spectra)])
    arrived = [exchange(slots, "stn", readers, d) for slots, d in zip(sent, distances)]

    table_shape = jax.ShapeDtypeStruct((freq_parts, chunks, 2 * LANES, QUARTER), jnp.bfloat16)
    high, low, own = pl.pallas_call(
        functools.partial(prepare_kernel, readers, hours * hour_parts),
        out_shape=[table_shape] * 2 + [slots_shape],
        in_specs=[smem, vmem, vmem],
        out_specs=[vmem] * 3,
        compiler_params=limit,
        cost_estimate=pl.CostEstimate(flops=5_000_000, bytes_accessed=2_000_000, transcendentals=0),
        name="own_slots_and_table",
    )(wanted, uptime, spectra)

    cross = pl.pallas_call(
        functools.partial(cross_kernel, [*distances, 0], parts, freq_parts, stations // SB),
        out_shape=[jax.ShapeDtypeStruct((2, part_pairs, freq_loc), jnp.float32)] * parts,
        in_specs=[vmem] * (1 + readers),
        out_specs=[vmem] * parts,
        scratch_shapes=[
            pltpu.VMEM((2 * reader_blocks, chunks, hours, 2 * SB, LANES), jnp.float32)
        ],
        compiler_params=limit,
        name="cross",
    )(wanted, *arrived, own)
    summed = [cross[0]] + [
        exchange(cross[distance], ("hour", "freq"), parts, distance) for distance in range(1, parts)
    ]

    return pl.pallas_call(
        functools.partial(lags_kernel, parts, freq_parts),
        out_shape=jax.ShapeDtypeStruct((part_pairs, L), jnp.float32),
        in_specs=[vmem] * (2 + parts),
        out_specs=vmem,
        compiler_params=limit,
        name="lags",
    )(high, low, *summed)


def solution(mesh):
    sizes = (mesh.shape["stn"], mesh.shape["hour"], mesh.shape["freq"])
    in_specs = (
        P(("groups", "hour"), "stn", None, "freq"),
        P(("groups", "hour"), "stn"),
        P("groups", None),
    )
    out_specs = P(("groups", "stn", "hour", "freq"), None)
    return jax.shard_map(
        functools.partial(per_device, sizes),
        mesh=mesh,
        in_specs=in_specs,
        out_specs=out_specs,
        check_vma=False,
    )
```

time: 27.5 us -> 24.3 us (0.88)
  Pallas kernels: 9.07 us -> 4.67 us
  waiting for transfers between devices: 9.71 us -> 13.6 us
  local copies, waits for them, and re-layouts: 2.59 us -> 0.01 us
    pallas_call x3, Pallas kernels: 7.57 us -> 3.62 us  [the longest x1 1.78 us: per_device(): pl.pallas_call(functools.partial(send_kernel, readers, distances), out_sh...]
    ppermute x6, waiting for transfers between devices: 9.71 us -> 13.6 us  [exchange(): return lax.ppermute(x, axes, [(i, i ^ distance) for i in range(size)])]
    unnamed x6 -> x4, local copies, waits for them, and re-layouts: 2.59 us -> 0.01 us
    pallas_call x1, Pallas kernels: 1.49 us -> 1.05 us  [per_device(): pl.pallas_call(functools.partial(lags_kernel, parts, freq_parts), out_sha...]
  transfers between devices with their start and end apart: 6 -> 6, of which waited for: 3 -> 4; matrix products, arithmetic and copies ran while one was open for 0% -> 0% of each run, Pallas kernels for 19% -> 5%
where the time goes in v3:
time: 24.3 us; the launch traced here: 24.2 us
  waiting for transfers between devices  13.6 us (56%)
  starting transfers between devices  5.88 us (24%)
  Pallas kernels  4.67 us (19%)
    ppermute x6, waiting for transfers between devices, exchange(): return lax.ppermute(x, axes, [(i, i ^ distance) for i in range(size)])  13.6 us
    ppermute x6, starting transfers between devices, exchange(): return lax.ppermute(x, axes, [(i, i ^ distance) for i in range(size)])  5.88 us
    pallas_call x1, Pallas kernels, per_device(): pl.pallas_call(functools.partial(send_kernel, readers, distances), out_sh...  1.78 us
    pallas_call x1, Pallas kernels, per_device(): pl.pallas_call(functools.partial(prepare_kernel, readers, hours * hour_pa...  1.22 us
    pallas_call x1, Pallas kernels, per_device(): pl.pallas_call(functools.partial(lags_kernel, parts, freq_parts), out_sha...  1.05 us
    pallas_call x1, Pallas kernels, per_device(): pl.pallas_call(functools.partial(cross_kernel, [*distances, 0], parts, fr...  0.61 us
  transfers between devices with their start and end apart: 6, of which 4 were waited for; matrix products, arithmetic and copies ran while one was open for 0% of the time, Pallas kernels for 5%

profile of v3, /device:TPU:21, one launch (start us, length us, event | category | flops | bytes accessed | tf_op | source)
XLA Modules:
  0.0 24.2 jit_solution(12042827500029494371)
XLA Ops:
  0.0 0.0 copy-start
  0.0 1.8 %send_slots.1 = (bf16[2,8,16,256]{3,2,1,0:T(8,128)(2,1)S(1)}, bf16[2,8,16,256]{3,2,1,0:T(8,128)(2,1)S(1)}, bf16[2,8,16,256]{3,2,1,0:T(8,128)(2,1)S(1)}, s32[2,8]{1,0:T(2,128)S(1)}) custom-call(s32[2,8]{1,0:T(2,128)} %bitcast.1, s32[8,128]{1,0:T(8,128)} %uptime_ref.1, bf16[8,128,2,256]{3,2,1,0:T(2,128)(2,1)} %spectra_ref.1), custom_call_target="tpu_custom_call" | custom-call | tf_op jit(solution)/shard_map/send_slots/pallas_call | solution.py:244
  1.8 0.0 copy-start.1
  1.8 0.1 collective-permute-start
  1.9 2.4 %collective-permute-start.1 = (bf16[2,8,16,256]{3,2,1,0:T(8,128)(2,1)S(1)}, bf16[2,8,16,256]{3,2,1,0:T(8,128)(2,1)S(1)}, u32[]{:S(2)}, u32[]{:S(2)}) collective-permute-start(bf16[2,8,16,256]{3,2,1,0:T(8,128)(2,1)S(1)} %get-tuple-element.20), channel_id=1, source_target_pairs={{0,12},{4,8},{8,4},{12,0},{1,13},{5,9},{9,5},{13,1},{2,14},{6,10},... | collective-permute-start | bytes 393224 | tf_op jit(solution)/shard_map/ppermute | solution.py:19
  4.3 1.1 %collective-permute-start.2 = (bf16[2,8,16,256]{3,2,1,0:T(8,128)(2,1)S(1)}, bf16[2,8,16,256]{3,2,1,0:T(8,128)(2,1)S(1)}, u32[]{:S(2)}, u32[]{:S(2)}) collective-permute-start(bf16[2,8,16,256]{3,2,1,0:T(8,128)(2,1)S(1)} %get-tuple-element.21), channel_id=1, source_target_pairs={{0,4},{4,0},{8,12},{12,8},{1,5},{5,1},{9,13},{13,9},{2,6},{6,2},{1... | collective-permute-start | bytes 393224 | tf_op jit(solution)/shard_map/ppermute | solution.py:19
  5.4 0.0 copy-done
  5.4 0.0 copy-done.1
  5.4 1.2 %own_slots_and_table.1 = (bf16[2,2,256,256]{3,2,1,0:T(8,128)(2,1)S(1)}, bf16[2,2,256,256]{3,2,1,0:T(8,128)(2,1)S(1)}, bf16[2,8,16,256]{3,2,1,0:T(8,128)(2,1)S(1)}) custom-call(s32[2,8]{1,0:T(2,128)S(1)} %get-tuple-element.16.pairs_ref, s32[8,128]{1,0:T(8,128)S(1)} %copy-done.1, bf16[8,128,2,256]{3,2,1,0:T(2,128)(2,1)S(1)} %copy-done), custom_call_target="tpu_custom_call" | custom-call | flops 5000000 | bytes 2000000 | tf_op jit(solution)/shard_map/own_slots_and_table/pallas_call | solution.py:261
  6.7 2.5 %collective-permute-done.refs_0_ = bf16[2,8,16,256]{3,2,1,0:T(8,128)(2,1)S(1)} collective-permute-done((bf16[2,8,16,256]{3,2,1,0:T(8,128)(2,1)S(1)}, bf16[2,8,16,256]{3,2,1,0:T(8,128)(2,1)S(1)}, u32[]{:S(2)}, u32[]{:S(2)}) %collective-permute-start) | collective-permute-done | bytes 131104 | tf_op jit(solution)/shard_map/ppermute | solution.py:19
  9.1 7.5 %collective-permute-done.1.refs_1_ = bf16[2,8,16,256]{3,2,1,0:T(8,128)(2,1)S(1)} collective-permute-done((bf16[2,8,16,256]{3,2,1,0:T(8,128)(2,1)S(1)}, bf16[2,8,16,256]{3,2,1,0:T(8,128)(2,1)S(1)}, u32[]{:S(2)}, u32[]{:S(2)}) %collective-permute-start.1) | collective-permute-done | bytes 131104 | tf_op jit(solution)/shard_map/ppermute | solution.py:19
  16.7 0.0 collective-permute-done.2.refs_2_
  16.7 0.6 %cross.1 = (f32[2,32,256]{2,1,0:T(8,128)S(1)}, f32[2,32,256]{2,1,0:T(8,128)S(1)}, f32[2,32,256]{2,1,0:T(8,128)S(1)}, f32[2,32,256]{2,1,0:T(8,128)S(1)}) custom-call(s32[2,8]{1,0:T(2,128)S(1)} %get-tuple-element.16.pairs_ref, bf16[2,8,16,256]{3,2,1,0:T(8,128)(2,1)S(1)} %collective-permute-done.refs_0_, ...), custom_call_target="tpu_custom_call" | custom-call | tf_op jit(solution)/shard_map/cross/pallas_call | solution.py:271
  17.3 0.6 %collective-permute-start.3 = (f32[2,32,256]{2,1,0:T(8,128)S(1)}, f32[2,32,256]{2,1,0:T(8,128)S(1)}, u32[]{:S(2)}, u32[]{:S(2)}) collective-permute-start(f32[2,32,256]{2,1,0:T(8,128)S(1)} %get-tuple-element.24), channel_id=1, source_target_pairs={{0,1},{1,0},{2,3},{3,2},{4,5},{5,4},{6,7},{7,6},{8,9},{9,8},{10,11... | collective-permute-start | bytes 196616 | tf_op jit(solution)/shard_map/ppermute | solution.py:19
  17.8 1.2 %collective-permute-start.4 = (f32[2,32,256]{2,1,0:T(8,128)S(1)}, f32[2,32,256]{2,1,0:T(8,128)S(1)}, u32[]{:S(2)}, u32[]{:S(2)}) collective-permute-start(f32[2,32,256]{2,1,0:T(8,128)S(1)} %get-tuple-element.25), channel_id=1, source_target_pairs={{0,2},{1,3},{2,0},{3,1},{4,6},{5,7},{6,4},{7,5},{8,10},{9,11},{10,... | collective-permute-start | bytes 196616 | tf_op jit(solution)/shard_map/ppermute | solution.py:19
  19.1 0.5 %collective-permute-start.5 = (f32[2,32,256]{2,1,0:T(8,128)S(1)}, f32[2,32,256]{2,1,0:T(8,128)S(1)}, u32[]{:S(2)}, u32[]{:S(2)}) collective-permute-start(f32[2,32,256]{2,1,0:T(8,128)S(1)} %get-tuple-element.26), channel_id=1, source_target_pairs={{0,3},{1,2},{2,1},{3,0},{4,7},{5,6},{6,5},{7,4},{8,11},{9,10},{10,... | collective-permute-start | bytes 196616 | tf_op jit(solution)/shard_map/ppermute | solution.py:19
  19.6 0.0 collective-permute-done.3.refs_1_
  19.6 2.0 %collective-permute-done.4.refs_2_ = f32[2,32,256]{2,1,0:T(8,128)S(1)} collective-permute-done((f32[2,32,256]{2,1,0:T(8,128)S(1)}, f32[2,32,256]{2,1,0:T(8,128)S(1)}, u32[]{:S(2)}, u32[]{:S(2)}) %collective-permute-start.4) | collective-permute-done | bytes 65568 | tf_op jit(solution)/shard_map/ppermute | solution.py:19
  21.5 1.6 %collective-permute-done.5.refs_3_ = f32[2,32,256]{2,1,0:T(8,128)S(1)} collective-permute-done((f32[2,32,256]{2,1,0:T(8,128)S(1)}, f32[2,32,256]{2,1,0:T(8,128)S(1)}, u32[]{:S(2)}, u32[]{:S(2)}) %collective-permute-start.5) | collective-permute-done | bytes 65568 | tf_op jit(solution)/shard_map/ppermute | solution.py:19
  23.1 1.0 %lags.1 = f32[32,1024]{1,0:T(8,128)} custom-call(bf16[2,2,256,256]{3,2,1,0:T(8,128)(2,1)S(1)} %get-tuple-element.17.high_ref, bf16[2,2,256,256]{3,2,1,0:T(8,128)(2,1)S(1)} %get-tuple-element.18.low_ref, f32[2,32,256]{2,1,0:T(8,128)S(1)} %get-tuple-element.23.refs_0_, f32[2,32,256]{2,1,0:T(8,128)S(1)} %collective-permute-done.3.refs_1_, ...), custom_call_target="tpu_custom_call" | custom-call | tf_op jit(solution)/shard_map/lags/pallas_call | solution.py:286
Async XLA Ops:
  0.0 5.4 %copy-start = (bf16[8,128,2,256]{3,2,1,0:T(2,128)(2,1)S(1)}, bf16[8,128,2,256]{3,2,1,0:T(2,128)(2,1)}, u32[]{:S(2)}) copy-start(bf16[8,128,2,256]{3,2,1,0:T(2,128)(2,1)} %spectra_ref.1) | copy-start | bytes 3145732
  1.8 3.6 %copy-start.1 = (s32[8,128]{1,0:T(8,128)S(1)}, s32[8,128]{1,0:T(8,128)}, u32[]{:S(2)}) copy-start(s32[8,128]{1,0:T(8,128)} %uptime_ref.1) | copy-start | bytes 12292
  1.8 7.3 %collective-permute-start = (bf16[2,8,16,256]{3,2,1,0:T(8,128)(2,1)S(1)}, bf16[2,8,16,256]{3,2,1,0:T(8,128)(2,1)S(1)}, u32[]{:S(2)}, u32[]{:S(2)}) collective-permute-start(bf16[2,8,16,256]{3,2,1,0:T(8,128)(2,1)S(1)} %get-tuple-element.19), channel_id=1, source_target_pairs={{0,8},{4,12},{8,0},{12,4},{1,9},{5,13},{9,1},{13,5},{2,10},{6,14},... | collective-permute-start | bytes 393224 | tf_op jit(solution)/shard_map/ppermute | solution.py:19
  1.9 14.7 %collective-permute-start.1 = (bf16[2,8,16,256]{3,2,1,0:T(8,128)(2,1)S(1)}, bf16[2,8,16,256]{3,2,1,0:T(8,128)(2,1)S(1)}, u32[]{:S(2)}, u32[]{:S(2)}) collective-permute-start(bf16[2,8,16,256]{3,2,1,0:T(8,128)(2,1)S(1)} %get-tuple-element.20), channel_id=1, source_target_pairs={{0,12},{4,8},{8,4},{12,0},{1,13},{5,9},{9,5},{13,1},{2,14},{6,10},... | collective-permute-start | bytes 393224 | tf_op jit(solution)/shard_map/ppermute | solution.py:19
  4.3 12.3 %collective-permute-start.2 = (bf16[2,8,16,256]{3,2,1,0:T(8,128)(2,1)S(1)}, bf16[2,8,16,256]{3,2,1,0:T(8,128)(2,1)S(1)}, u32[]{:S(2)}, u32[]{:S(2)}) collective-permute-start(bf16[2,8,16,256]{3,2,1,0:T(8,128)(2,1)S(1)} %get-tuple-element.21), channel_id=1, source_target_pairs={{0,4},{4,0},{8,12},{12,8},{1,5},{5,1},{9,13},{13,9},{2,6},{6,2},{1... | collective-permute-start | bytes 393224 | tf_op jit(solution)/shard_map/ppermute | solution.py:19
  17.3 2.3 %collective-permute-start.3 = (f32[2,32,256]{2,1,0:T(8,128)S(1)}, f32[2,32,256]{2,1,0:T(8,128)S(1)}, u32[]{:S(2)}, u32[]{:S(2)}) collective-permute-start(f32[2,32,256]{2,1,0:T(8,128)S(1)} %get-tuple-element.24), channel_id=1, source_target_pairs={{0,1},{1,0},{2,3},{3,2},{4,5},{5,4},{6,7},{7,6},{8,9},{9,8},{10,11... | collective-permute-start | bytes 196616 | tf_op jit(solution)/shard_map/ppermute | solution.py:19
  17.8 3.7 %collective-permute-start.4 = (f32[2,32,256]{2,1,0:T(8,128)S(1)}, f32[2,32,256]{2,1,0:T(8,128)S(1)}, u32[]{:S(2)}, u32[]{:S(2)}) collective-permute-start(f32[2,32,256]{2,1,0:T(8,128)S(1)} %get-tuple-element.25), channel_id=1, source_target_pairs={{0,2},{1,3},{2,0},{3,1},{4,6},{5,7},{6,4},{7,5},{8,10},{9,11},{10,... | collective-permute-start | bytes 196616 | tf_op jit(solution)/shard_map/ppermute | solution.py:19
  19.1 4.0 %collective-permute-start.5 = (f32[2,32,256]{2,1,0:T(8,128)S(1)}, f32[2,32,256]{2,1,0:T(8,128)S(1)}, u32[]{:S(2)}, u32[]{:S(2)}) collective-permute-start(f32[2,32,256]{2,1,0:T(8,128)S(1)} %get-tuple-element.26), channel_id=1, source_target_pairs={{0,3},{1,2},{2,1},{3,0},{4,7},{5,6},{6,5},{7,4},{8,11},{9,10},{10,... | collective-permute-start | bytes 196616 | tf_op jit(solution)/shard_map/ppermute | solution.py:19

commit v4 on v3

--- a/solution.py
+++ b/solution.py
@@ -13,6 +13,10 @@
 CAP = 2
 LANES = 128
 QUARTER = L // 4
+
+
+def shift(x, axis, size, distance):
+    return lax.ppermute(x, axis, [(i, (i + distance) % size) for i in range(size)])
 
 
 def exchange(x, axes, size, distance):
@@ -48,47 +52,44 @@
     return jnp.where(keep, values, 0.0).astype(jnp.bfloat16)
 
 
-def write_slots(pairs_ref, up, spectra_ref, readers, distances, hours_ready, out_refs):
+def send_kernel(readers, distances, pairs_hbm, uptime_hbm, spectra_hbm, *refs):
+    slot_refs, (pairs_ref, uptime_ref, spectra_ref, sems) = refs[:-4], refs[-4:]
     me = lax.axis_index("stn")
-    stations = up.shape[1]
+    hours, stations = uptime_ref.shape
     reader_blocks = pairs_ref.shape[1] // readers
-    wanted = []
-    for out_ref, distance in zip(out_refs, distances, strict=True):
-        starts = wanted_slots(pairs_ref, me ^ distance, me, reader_blocks, stations // SB)
-        for slot, start in enumerate(starts):
-            wanted.append((out_ref, slot, start, recorded_rows(start, up)))
-    for hour in range(spectra_ref.shape[0]):
-        if hours_ready is not None:
-            hours_ready[hour].wait()
-        for out_ref, slot, start, recorded in wanted:
-            out_ref[slot, hour] = masked_rows(spectra_ref, hour, start, recorded)
-
-
-def send_kernel(readers, distances, pairs_hbm, uptime_hbm, spectra_hbm, *refs):
-    out_refs, (pairs_out, pairs_ref, uptime_ref, spectra_ref, sems) = refs[:-5], refs[-5:]
     arguments = [
         pltpu.make_async_copy(pairs_hbm, pairs_ref, sems.at[0]),
         pltpu.make_async_copy(uptime_hbm, uptime_ref, sems.at[1]),
-        pltpu.make_async_copy(pairs_hbm, pairs_out, sems.at[2]),
     ]
-    spectra = [
-        pltpu.make_async_copy(spectra_hbm.at[h], spectra_ref.at[h], sems.at[3 + h])
-        for h in range(spectra_ref.shape[0])
-    ]
+    pieces = 2 if hours % 2 == 0 else 1
+    count = hours // pieces
+    spectra = []
+    for piece in range(pieces):
+        some = pl.ds(piece * count, count)
+        spectra.append(
+            pltpu.make_async_copy(spectra_hbm.at[some], spectra_ref.at[some], sems.at[2 + piece])
+        )
     for copy in arguments + spectra:
         copy.start()
     for copy in arguments:
         copy.wait()
     up = uptime_ref[...].astype(jnp.float32).astype(jnp.bfloat16)
-    write_slots(pairs_ref, up, spectra_ref, readers, distances, spectra, out_refs)
-
-
-def prepare_kernel(readers, hour_total, pairs_ref, uptime_ref, spectra_ref, *refs):
-    high_ref, low_ref, own_ref = refs
-    up = uptime_ref[...].astype(jnp.float32).astype(jnp.bfloat16)
-    write_slots(pairs_ref, up, spectra_ref, readers, [0], None, [own_ref])
-
-    _, chunks, _, lags = high_ref.shape
+    wanted = []
+    for slot_ref, distance in zip(slot_refs, distances, strict=True):
+        reader = (me + distance) % readers
+        starts = wanted_slots(pairs_ref, reader, me, reader_blocks, stations // SB)
+        for slot, start in enumerate(starts):
+            wanted.append((slot_ref, slot, start, recorded_rows(start, up)))
+    for hour in range(hours):
+        if hour % count == 0:
+            spectra[hour // count].wait()
+        for slot_ref, slot, start, recorded in wanted:
+            slot_ref[slot, hour] = masked_rows(spectra_ref, hour, start, recorded)
+
+
+def table_kernel(hour_total, wanted_ref, high_ref, low_ref):
+    del wanted_ref
+    _, rows, lags = high_ref.shape
     half = L // 2
     tall = 16
     groups = half // tall
@@ -110,15 +111,15 @@
         weight = weight * weight * scale
         cos0 = (base_cos * turn_cos - base_sin * turn_sin) * weight
         sin0 = (base_sin * turn_cos + base_cos * turn_sin) * weight
-        row = group % (LANES // tall) * tall
-        at = group // (LANES // tall)
+        chunk, row = divmod(group * tall, LANES)
+        at, chunk = divmod(chunk * 2 * LANES, rows)
         for j in range(lags // LANES):
             real, imag = cos0, -sin0
             if j > 0:
                 cj, sj = steps[j - 1]
                 real, imag = cos0 * cj - sin0 * sj, -(sin0 * cj + cos0 * sj)
-            for first, value in ((row, real), (LANES + row, imag)):
-                where = (at // chunks, at % chunks, pl.ds(first, tall), pl.ds(j * LANES, LANES))
+            for first, value in ((chunk + row, real), (chunk + LANES + row, imag)):
+                where = (at, pl.ds(first, tall), pl.ds(j * LANES, LANES))
                 high = value.astype(jnp.bfloat16)
                 high_ref[where] = high
                 low_ref[where] = (value - high.astype(jnp.float32)).astype(jnp.bfloat16)
@@ -147,13 +148,9 @@
     mine = lax.axis_index("hour") * freq_parts + lax.axis_index("freq")
     reader_blocks = pairs_ref.shape[1] // readers
     _, chunks, hours, _, _ = blocks.shape
-    pairs = pairs_ref[...]
-    side = lax.broadcasted_iota(jnp.int32, pairs.shape, 0)
-    column = lax.broadcasted_iota(jnp.int32, pairs.shape, 1)
     wanted = []
     for entry in range(2 * reader_blocks):
-        here = (side == entry % 2) & (column == me * reader_blocks + entry // 2)
-        wanted.append(jnp.max(jnp.where(here, pairs, 0)))
+        wanted.append(pairs_ref[entry % 2, me * reader_blocks + entry // 2])
     owners = [block // owned for block in wanted]
     for entry in range(2 * reader_blocks):
         slot = jnp.int32(0)
@@ -162,7 +159,7 @@
         slot = jnp.minimum(slot, CAP - 1)
         for slot_ref, distance in zip(slot_refs, distances, strict=True):
 
-            @pl.when(owners[entry] == me ^ distance)
+            @pl.when(owners[entry] == (me + readers - distance) % readers)
             def _(entry=entry, slot=slot, slot_ref=slot_ref):
                 values = slot_ref[slot].astype(jnp.float32)
                 for chunk in range(chunks):
@@ -194,10 +191,12 @@
     part_refs, out_ref = refs[:-1], refs[-1]
     own = lax.axis_index("freq")
     count = out_ref.shape[0]
+    chunks = part_refs[0].shape[2] // LANES
     phase = lax.broadcasted_iota(jnp.int32, (count, LANES), 1) % 4
     total = None
     for c in range(freq_parts):
-        for chunk in range(high_ref.shape[1]):
+        highs, lows = [], []
+        for chunk in range(chunks):
             lanes = pl.ds(chunk * LANES, LANES)
             cross = part_refs[c][:, :, lanes]
             for x in range(1, parts // freq_parts):
@@ -213,14 +212,14 @@
                 turned.append(jnp.concatenate([re, im], axis=1))
             turned = jnp.concatenate(turned, axis=0)
             high = turned.astype(jnp.bfloat16)
-            low = (turned - high.astype(jnp.float32)).astype(jnp.bfloat16)
-            table_high = high_ref[own ^ c, chunk]
-            term = (
-                jnp.dot(high, table_high, preferred_element_type=jnp.float32)
-                + jnp.dot(low, table_high, preferred_element_type=jnp.float32)
-                + jnp.dot(high, low_ref[own ^ c, chunk], preferred_element_type=jnp.float32)
-            )
-            total = term if total is None else total + term
+            highs.append(high)
+            lows.append((turned - high.astype(jnp.float32)).astype(jnp.bfloat16))
+        high, low = jnp.concatenate(highs, axis=1), jnp.concatenate(lows, axis=1)
+        both = jnp.concatenate([high, low], axis=0)
+        by_high = jnp.dot(both, high_ref[own ^ c], preferred_element_type=jnp.float32)
+        by_low = jnp.dot(high, low_ref[own ^ c], preferred_element_type=jnp.float32)
+        term = by_high[: 4 * count] + (by_high[4 * count :] + by_low)
+        total = term if total is None else total + term
     for q in range(4):
         out_ref[:, q * QUARTER : (q + 1) * QUARTER] = total[q * count : (q + 1) * count]
 
@@ -238,47 +237,45 @@
     hbm = pl.BlockSpec(memory_space=pltpu.HBM)
     limit = pltpu.CompilerParams(vmem_limit_bytes=32 * 1024 * 1024)
     slots_shape = jax.ShapeDtypeStruct((CAP, hours, 2 * SB, freq_loc), jnp.bfloat16)
-    pairs_shape = jax.ShapeDtypeStruct(pairs.shape, jnp.int32)
-
-    distances = [*range(readers // 2, readers), *range(1, readers // 2)]
-    *sent, wanted = pl.pallas_call(
-        functools.partial(send_kernel, readers, distances),
-        out_shape=[slots_shape] * len(distances) + [pairs_shape],
+
+    distances = sorted(range(1, readers), key=lambda d: (abs(2 * d - readers), -d))
+    *sent, own, wanted = pl.pallas_call(
+        functools.partial(send_kernel, readers, [*distances, 0]),
+        out_shape=[slots_shape] * (len(distances) + 1) + [pltpu.SMEM(pairs.shape, jnp.int32)],
         in_specs=[hbm] * 3,
-        out_specs=[vmem] * (len(distances) + 1),
+        out_specs=[vmem] * (len(distances) + 1) + [smem],
         scratch_shapes=[
-            pltpu.SMEM(pairs.shape, jnp.int32),
             pltpu.VMEM(uptime.shape, jnp.int32),
             pltpu.VMEM(spectra.shape, jnp.bfloat16),
-            pltpu.SemaphoreType.DMA((3 + hours,)),
+            pltpu.SemaphoreType.DMA((4,)),
         ],
         compiler_params=limit,
         name="send_slots",
     )(*[pltpu.with_memory_space_constraint(x, pltpu.HBM) for x in (pairs, uptime, spectra)])
-    arrived = [exchange(slots, "stn", readers, d) for slots, d in zip(sent, distances)]
-
-    table_shape = jax.ShapeDtypeStruct((freq_parts, chunks, 2 * LANES, QUARTER), jnp.bfloat16)
-    high, low, own = pl.pallas_call(
-        functools.partial(prepare_kernel, readers, hours * hour_parts),
-        out_shape=[table_shape] * 2 + [slots_shape],
-        in_specs=[smem, vmem, vmem],
-        out_specs=[vmem] * 3,
+    arrived = [shift(slots, "stn", readers, d) for slots, d in zip(sent, distances)]
+
+    table_shape = jax.ShapeDtypeStruct((freq_parts, 2 * freq_loc, QUARTER), jnp.bfloat16)
+    high, low = pl.pallas_call(
+        functools.partial(table_kernel, hours * hour_parts),
+        out_shape=[table_shape] * 2,
+        in_specs=[smem],
+        out_specs=[vmem] * 2,
         compiler_params=limit,
         cost_estimate=pl.CostEstimate(flops=5_000_000, bytes_accessed=2_000_000, transcendentals=0),
-        name="own_slots_and_table",
-    )(wanted, uptime, spectra)
+        name="band_table",
+    )(pltpu.with_memory_space_constraint(wanted, pltpu.SMEM))
 
     cross = pl.pallas_call(
         functools.partial(cross_kernel, [*distances, 0], parts, freq_parts, stations // SB),
         out_shape=[jax.ShapeDtypeStruct((2, part_pairs, freq_loc), jnp.float32)] * parts,
-        in_specs=[vmem] * (1 + readers),
+        in_specs=[smem] + [vmem] * readers,
         out_specs=[vmem] * parts,
         scratch_shapes=[
             pltpu.VMEM((2 * reader_blocks, chunks, hours, 2 * SB, LANES), jnp.float32)
         ],
         compiler_params=limit,
         name="cross",
-    )(wanted, *arrived, own)
+    )(pltpu.with_memory_space_constraint(wanted, pltpu.SMEM), *arrived, own)
     summed = [cross[0]] + [
         exchange(cross[distance], ("hour", "freq"), parts, distance) for distance in range(1, parts)
     ]

time: 24.3 us -> 23.7 us (0.975)
  the two profiles are of different devices: /device:TPU:21 before, /device:TPU:17 now
where the time goes in v4:
time: 23.7 us; the launch traced here: 23.5 us
  waiting for transfers between devices  15.4 us (65%)
  starting transfers between devices  4.81 us (20%)
  Pallas kernels  3.29 us (14%)
    ppermute x3, waiting for transfers between devices, shift(): lax.ppermute(x, axis, [(i, (i + distance) % size) for i in range(size)])  12.3 us
    ppermute x3, waiting for transfers between devices, exchange(): return lax.ppermute(x, axes, [(i, i ^ distance) for i in range(size)])  3.08 us
    ppermute x3, starting transfers between devices, shift(): lax.ppermute(x, axis, [(i, (i + distance) % size) for i in range(size)])  2.54 us
    ppermute x3, starting transfers between devices, exchange(): return lax.ppermute(x, axes, [(i, i ^ distance) for i in range(size)])  2.27 us
    pallas_call x1, Pallas kernels, per_device(): pl.pallas_call(functools.partial(send_kernel, readers, [*distances, 0]),...  1.4 us
    pallas_call x1, Pallas kernels, per_device(): pl.pallas_call(functools.partial(lags_kernel, parts, freq_parts), out_sha...  1.04 us
  transfers between devices with their start and end apart: 6, of which 5 were waited for; matrix products, arithmetic and copies ran while one was open for 0% of the time, Pallas kernels for 2%

profile of v4, /device:TPU:17, one launch (start us, length us, event | category | flops | bytes accessed | tf_op | source)
XLA Modules:
  0.0 23.5 jit_solution(12092028475289546621)
XLA Ops:
  0.0 1.4 %send_slots.1 = (bf16[2,8,16,256]{3,2,1,0:T(8,128)(2,1)S(1)}, bf16[2,8,16,256]{3,2,1,0:T(8,128)(2,1)S(1)}, bf16[2,8,16,256]{3,2,1,0:T(8,128)(2,1)S(1)}, bf16[2,8,16,256]{3,2,1,0:T(8,128)(2,1)S(1)}, s32[2,8]{1,0:T(2,128)S(4)}) custom-call(s32[2,8]{1,0:T(2,128)} %bitcast.1, s32[8,128]{1,0:T(8,128)} %uptime_hbm.1, bf16[8,128,2,256]{3,2,1,0:T(2,128)(2,1)} %spectra_hbm.1), custom_call_target="tpu_custom_call" | custom-call | tf_op jit(solution)/shard_map/send_slots/pallas_call | solution.py:242
  1.4 0.1 collective-permute-start
  1.5 2.5 %collective-permute-start.1 = (bf16[2,8,16,256]{3,2,1,0:T(8,128)(2,1)S(1)}, bf16[2,8,16,256]{3,2,1,0:T(8,128)(2,1)S(1)}, u32[]{:S(2)}, u32[]{:S(2)}) collective-permute-start(bf16[2,8,16,256]{3,2,1,0:T(8,128)(2,1)S(1)} %get-tuple-element.20), channel_id=1, source_target_pairs={{0,12},{4,0},{8,4},{12,8},{1,13},{5,1},{9,5},{13,9},{2,14},{6,2},{... | collective-permute-start | bytes 393224 | tf_op jit(solution)/shard_map/ppermute | solution.py:19
  4.0 0.0 collective-permute-start.2
  4.0 2.8 %collective-permute-done.refs_0_ = bf16[2,8,16,256]{3,2,1,0:T(8,128)(2,1)S(1)} collective-permute-done((bf16[2,8,16,256]{3,2,1,0:T(8,128)(2,1)S(1)}, bf16[2,8,16,256]{3,2,1,0:T(8,128)(2,1)S(1)}, u32[]{:S(2)}, u32[]{:S(2)}) %collective-permute-start) | collective-permute-done | bytes 131104 | tf_op jit(solution)/shard_map/ppermute | solution.py:19
  6.7 5.5 %collective-permute-done.1.refs_1_ = bf16[2,8,16,256]{3,2,1,0:T(8,128)(2,1)S(1)} collective-permute-done((bf16[2,8,16,256]{3,2,1,0:T(8,128)(2,1)S(1)}, bf16[2,8,16,256]{3,2,1,0:T(8,128)(2,1)S(1)}, u32[]{:S(2)}, u32[]{:S(2)}) %collective-permute-start.1) | collective-permute-done | bytes 131104 | tf_op jit(solution)/shard_map/ppermute | solution.py:19
  12.2 4.0 %collective-permute-done.2.refs_2_ = bf16[2,8,16,256]{3,2,1,0:T(8,128)(2,1)S(1)} collective-permute-done((bf16[2,8,16,256]{3,2,1,0:T(8,128)(2,1)S(1)}, bf16[2,8,16,256]{3,2,1,0:T(8,128)(2,1)S(1)}, u32[]{:S(2)}, u32[]{:S(2)}) %collective-permute-start.2) | collective-permute-done | bytes 131104 | tf_op jit(solution)/shard_map/ppermute | solution.py:19
  16.3 0.4 %cross.1 = (f32[2,32,256]{2,1,0:T(8,128)S(1)}, f32[2,32,256]{2,1,0:T(8,128)S(1)}, f32[2,32,256]{2,1,0:T(8,128)S(1)}, f32[2,32,256]{2,1,0:T(8,128)S(1)}) custom-call(s32[2,8]{1,0:T(2,128)S(4)} %get-tuple-element.16.wanted_ref.pairs_ref, bf16[2,8,16,256]{3,2,1,0:T(8,128)(2,1)S(1)} %collective-permute-done.refs_0_, ...), custom_call_target="tpu_custom_call" | custom-call | tf_op jit(solution)/shard_map/cross/pallas_call | solution.py:268
  16.6 0.6 %collective-permute-start.3 = (f32[2,32,256]{2,1,0:T(8,128)S(1)}, f32[2,32,256]{2,1,0:T(8,128)S(1)}, u32[]{:S(2)}, u32[]{:S(2)}) collective-permute-start(f32[2,32,256]{2,1,0:T(8,128)S(1)} %get-tuple-element.24), channel_id=1, source_target_pairs={{0,1},{1,0},{2,3},{3,2},{4,5},{5,4},{6,7},{7,6},{8,9},{9,8},{10,11... | collective-permute-start | bytes 196616 | tf_op jit(solution)/shard_map/ppermute | solution.py:23
  17.2 1.2 %collective-permute-start.4 = (f32[2,32,256]{2,1,0:T(8,128)S(1)}, f32[2,32,256]{2,1,0:T(8,128)S(1)}, u32[]{:S(2)}, u32[]{:S(2)}) collective-permute-start(f32[2,32,256]{2,1,0:T(8,128)S(1)} %get-tuple-element.25), channel_id=1, source_target_pairs={{0,2},{1,3},{2,0},{3,1},{4,6},{5,7},{6,4},{7,5},{8,10},{9,11},{10,... | collective-permute-start | bytes 196616 | tf_op jit(solution)/shard_map/ppermute | solution.py:23
  18.4 0.5 %collective-permute-start.5 = (f32[2,32,256]{2,1,0:T(8,128)S(1)}, f32[2,32,256]{2,1,0:T(8,128)S(1)}, u32[]{:S(2)}, u32[]{:S(2)}) collective-permute-start(f32[2,32,256]{2,1,0:T(8,128)S(1)} %get-tuple-element.26), channel_id=1, source_target_pairs={{0,3},{1,2},{2,1},{3,0},{4,7},{5,6},{6,5},{7,4},{8,11},{9,10},{10,... | collective-permute-start | bytes 196616 | tf_op jit(solution)/shard_map/ppermute | solution.py:23
  18.9 0.5 %band_table.1 = (bf16[2,512,256]{2,1,0:T(8,128)(2,1)S(1)}, bf16[2,512,256]{2,1,0:T(8,128)(2,1)S(1)}) custom-call(s32[2,8]{1,0:T(2,128)S(4)} %get-tuple-element.16.wanted_ref.pairs_ref), custom_call_target="tpu_custom_call" | custom-call | flops 5000000 | bytes 2000000 | tf_op jit(solution)/shard_map/band_table/pallas_call | solution.py:258
  19.4 0.0 collective-permute-done.3.refs_1_
  19.4 1.5 %collective-permute-done.4.refs_2_ = f32[2,32,256]{2,1,0:T(8,128)S(1)} collective-permute-done((f32[2,32,256]{2,1,0:T(8,128)S(1)}, f32[2,32,256]{2,1,0:T(8,128)S(1)}, u32[]{:S(2)}, u32[]{:S(2)}) %collective-permute-start.4) | collective-permute-done | bytes 65568 | tf_op jit(solution)/shard_map/ppermute | solution.py:23
  20.9 1.6 %collective-permute-done.5.refs_3_ = f32[2,32,256]{2,1,0:T(8,128)S(1)} collective-permute-done((f32[2,32,256]{2,1,0:T(8,128)S(1)}, f32[2,32,256]{2,1,0:T(8,128)S(1)}, u32[]{:S(2)}, u32[]{:S(2)}) %collective-permute-start.5) | collective-permute-done | bytes 65568 | tf_op jit(solution)/shard_map/ppermute | solution.py:23
  22.5 1.0 %lags.1 = f32[32,1024]{1,0:T(8,128)} custom-call(bf16[2,512,256]{2,1,0:T(8,128)(2,1)S(1)} %get-tuple-element.17.high_ref, bf16[2,512,256]{2,1,0:T(8,128)(2,1)S(1)} %get-tuple-element.18.low_ref, f32[2,32,256]{2,1,0:T(8,128)S(1)} %get-tuple-element.23.refs_0_, f32[2,32,256]{2,1,0:T(8,128)S(1)} %collective-permute-done.3.refs_1_, ...), custom_call_target="tpu_custom_call" | custom-call | tf_op jit(solution)/shard_map/lags/pallas_call | solution.py:283
Async XLA Ops:
  1.4 5.3 %collective-permute-start = (bf16[2,8,16,256]{3,2,1,0:T(8,128)(2,1)S(1)}, bf16[2,8,16,256]{3,2,1,0:T(8,128)(2,1)S(1)}, u32[]{:S(2)}, u32[]{:S(2)}) collective-permute-start(bf16[2,8,16,256]{3,2,1,0:T(8,128)(2,1)S(1)} %get-tuple-element.19), channel_id=1, source_target_pairs={{0,8},{4,12},{8,0},{12,4},{1,9},{5,13},{9,1},{13,5},{2,10},{6,14},... | collective-permute-start | bytes 393224 | tf_op jit(solution)/shard_map/ppermute | solution.py:19
  1.5 10.8 %collective-permute-start.1 = (bf16[2,8,16,256]{3,2,1,0:T(8,128)(2,1)S(1)}, bf16[2,8,16,256]{3,2,1,0:T(8,128)(2,1)S(1)}, u32[]{:S(2)}, u32[]{:S(2)}) collective-permute-start(bf16[2,8,16,256]{3,2,1,0:T(8,128)(2,1)S(1)} %get-tuple-element.20), channel_id=1, source_target_pairs={{0,12},{4,0},{8,4},{12,8},{1,13},{5,1},{9,5},{13,9},{2,14},{6,2},{... | collective-permute-start | bytes 393224 | tf_op jit(solution)/shard_map/ppermute | solution.py:19
  4.0 12.3 %collective-permute-start.2 = (bf16[2,8,16,256]{3,2,1,0:T(8,128)(2,1)S(1)}, bf16[2,8,16,256]{3,2,1,0:T(8,128)(2,1)S(1)}, u32[]{:S(2)}, u32[]{:S(2)}) collective-permute-start(bf16[2,8,16,256]{3,2,1,0:T(8,128)(2,1)S(1)} %get-tuple-element.21), channel_id=1, source_target_pairs={{0,4},{4,8},{8,12},{12,0},{1,5},{5,9},{9,13},{13,1},{2,6},{6,10},{... | collective-permute-start | bytes 393224 | tf_op jit(solution)/shard_map/ppermute | solution.py:19
  16.6 2.7 %collective-permute-start.3 = (f32[2,32,256]{2,1,0:T(8,128)S(1)}, f32[2,32,256]{2,1,0:T(8,128)S(1)}, u32[]{:S(2)}, u32[]{:S(2)}) collective-permute-start(f32[2,32,256]{2,1,0:T(8,128)S(1)} %get-tuple-element.24), channel_id=1, source_target_pairs={{0,1},{1,0},{2,3},{3,2},{4,5},{5,4},{6,7},{7,6},{8,9},{9,8},{10,11... | collective-permute-start | bytes 196616 | tf_op jit(solution)/shard_map/ppermute | solution.py:23
  17.2 3.7 %collective-permute-start.4 = (f32[2,32,256]{2,1,0:T(8,128)S(1)}, f32[2,32,256]{2,1,0:T(8,128)S(1)}, u32[]{:S(2)}, u32[]{:S(2)}) collective-permute-start(f32[2,32,256]{2,1,0:T(8,128)S(1)} %get-tuple-element.25), channel_id=1, source_target_pairs={{0,2},{1,3},{2,0},{3,1},{4,6},{5,7},{6,4},{7,5},{8,10},{9,11},{10,... | collective-permute-start | bytes 196616 | tf_op jit(solution)/shard_map/ppermute | solution.py:23
  18.4 4.0 %collective-permute-start.5 = (f32[2,32,256]{2,1,0:T(8,128)S(1)}, f32[2,32,256]{2,1,0:T(8,128)S(1)}, u32[]{:S(2)}, u32[]{:S(2)}) collective-permute-start(f32[2,32,256]{2,1,0:T(8,128)S(1)} %get-tuple-element.26), channel_id=1, source_target_pairs={{0,3},{1,2},{2,1},{3,0},{4,7},{5,6},{6,5},{7,4},{8,11},{9,10},{10,... | collective-permute-start | bytes 196616 | tf_op jit(solution)/shard_map/ppermute | solution.py:23

commit v5 on v4

--- a/solution.py
+++ b/solution.py
@@ -15,8 +15,17 @@
 QUARTER = L // 4
 
 
-def shift(x, axis, size, distance):
-    return lax.ppermute(x, axis, [(i, (i + distance) % size) for i in range(size)])
+def station_rounds(readers):
+    ring = [i // 2 if i % 2 == 0 else readers - 1 - i // 2 for i in range(readers)]
+    shifts = [*range(1, readers, 2), *range(2, readers, 2)]
+    return [[ring[(ring.index(s) + d) % readers] for s in range(readers)] for d in shifts]
+
+
+def pick(table, index):
+    value = jnp.int32(table[0])
+    for position, entry in enumerate(table):
+        value = jnp.where(index == position, jnp.int32(entry), value)
+    return value
 
 
 def exchange(x, axes, size, distance):
@@ -52,7 +61,7 @@
     return jnp.where(keep, values, 0.0).astype(jnp.bfloat16)
 
 
-def send_kernel(readers, distances, pairs_hbm, uptime_hbm, spectra_hbm, *refs):
+def send_kernel(readers, rounds, pairs_hbm, uptime_hbm, spectra_hbm, *refs):
     slot_refs, (pairs_ref, uptime_ref, spectra_ref, sems) = refs[:-4], refs[-4:]
     me = lax.axis_index("stn")
     hours, stations = uptime_ref.shape
@@ -75,8 +84,8 @@
         copy.wait()
     up = uptime_ref[...].astype(jnp.float32).astype(jnp.bfloat16)
     wanted = []
-    for slot_ref, distance in zip(slot_refs, distances, strict=True):
-        reader = (me + distance) % readers
+    for slot_ref, targets in zip(slot_refs, rounds, strict=True):
+        reader = pick(targets, me)
         starts = wanted_slots(pairs_ref, reader, me, reader_blocks, stations // SB)
         for slot, start in enumerate(starts):
             wanted.append((slot_ref, slot, start, recorded_rows(start, up)))
@@ -141,9 +150,10 @@
     return out_cos, out_sin
 
 
-def cross_kernel(distances, parts, freq_parts, owned, pairs_ref, *refs):
-    readers = len(distances)
-    slot_refs, out_refs, blocks = refs[:readers], refs[readers : readers + parts], refs[-1]
+def cross_kernel(rounds, parts, freq_parts, owned, pairs_ref, *refs):
+    readers = len(rounds[0])
+    count = len(rounds)
+    slot_refs, out_refs, blocks = refs[:count], refs[count : count + parts], refs[-1]
     me = lax.axis_index("stn")
     mine = lax.axis_index("hour") * freq_parts + lax.axis_index("freq")
     reader_blocks = pairs_ref.shape[1] // readers
@@ -157,9 +167,9 @@
         for before in range(entry):
             slot = slot + (owners[before] == owners[entry]).astype(jnp.int32)
         slot = jnp.minimum(slot, CAP - 1)
-        for slot_ref, distance in zip(slot_refs, distances, strict=True):
-
-            @pl.when(owners[entry] == (me + readers - distance) % readers)
+        for slot_ref, sources in zip(slot_refs, rounds, strict=True):
+
+            @pl.when(owners[entry] == pick(sources, me))
             def _(entry=entry, slot=slot, slot_ref=slot_ref):
                 values = slot_ref[slot].astype(jnp.float32)
                 for chunk in range(chunks):
@@ -238,12 +248,13 @@
     limit = pltpu.CompilerParams(vmem_limit_bytes=32 * 1024 * 1024)
     slots_shape = jax.ShapeDtypeStruct((CAP, hours, 2 * SB, freq_loc), jnp.bfloat16)
 
-    distances = sorted(range(1, readers), key=lambda d: (abs(2 * d - readers), -d))
+    rounds = station_rounds(readers)
+    here = [*range(readers)]
     *sent, own, wanted = pl.pallas_call(
-        functools.partial(send_kernel, readers, [*distances, 0]),
-        out_shape=[slots_shape] * (len(distances) + 1) + [pltpu.SMEM(pairs.shape, jnp.int32)],
+        functools.partial(send_kernel, readers, [*rounds, here]),
+        out_shape=[slots_shape] * (len(rounds) + 1) + [pltpu.SMEM(pairs.shape, jnp.int32)],
         in_specs=[hbm] * 3,
-        out_specs=[vmem] * (len(distances) + 1) + [smem],
+        out_specs=[vmem] * (len(rounds) + 1) + [smem],
         scratch_shapes=[
             pltpu.VMEM(uptime.shape, jnp.int32),
             pltpu.VMEM(spectra.shape, jnp.bfloat16),
@@ -252,7 +263,11 @@
         compiler_params=limit,
         name="send_slots",
     )(*[pltpu.with_memory_space_constraint(x, pltpu.HBM) for x in (pairs, uptime, spectra)])
-    arrived = [shift(slots, "stn", readers, d) for slots, d in zip(sent, distances)]
+    arrived = [
+        lax.ppermute(slots, "stn", [*enumerate(targets)])
+        for slots, targets in zip(sent, rounds, strict=True)
+    ]
+    sources = [[targets.index(t) for t in range(readers)] for targets in rounds]
 
     table_shape = jax.ShapeDtypeStruct((freq_parts, 2 * freq_loc, QUARTER), jnp.bfloat16)
     high, low = pl.pallas_call(
@@ -266,9 +281,9 @@
     )(pltpu.with_memory_space_constraint(wanted, pltpu.SMEM))
 
     cross = pl.pallas_call(
-        functools.partial(cross_kernel, [*distances, 0], parts, freq_parts, stations // SB),
+        functools.partial(cross_kernel, [*sources, here], parts, freq_parts, stations // SB),
         out_shape=[jax.ShapeDtypeStruct((2, part_pairs, freq_loc), jnp.float32)] * parts,
-        in_specs=[smem] + [vmem] * readers,
+        in_specs=[smem] + [vmem] * (len(rounds) + 1),
         out_specs=[vmem] * parts,
         scratch_shapes=[
             pltpu.VMEM((2 * reader_blocks, chunks, hours, 2 * SB, LANES), jnp.float32)

time: 23.7 us -> 23.2 us (0.979)
  the two profiles are of different devices: /device:TPU:17 before, /device:TPU:0 now
where the time goes in v5:
time: 23.2 us; the launch traced here: 23.1 us
  waiting for transfers between devices  11.8 us (51%)
  starting transfers between devices  7.93 us (34%)
  Pallas kernels  3.31 us (14%)
    ppermute x3, waiting for transfers between devices, per_device(): lax.ppermute(slots, 'stn', [*enumerate(targets)])  8.52 us
    ppermute x3, starting transfers between devices, per_device(): lax.ppermute(slots, 'stn', [*enumerate(targets)])  6 us
    ppermute x3, waiting for transfers between devices, exchange(): return lax.ppermute(x, axes, [(i, i ^ distance) for i in range(size)])  3.31 us
    ppermute x3, starting transfers between devices, exchange(): return lax.ppermute(x, axes, [(i, i ^ distance) for i in range(size)])  1.93 us
    pallas_call x1, Pallas kernels, per_device(): pl.pallas_call(functools.partial(send_kernel, readers, [*rounds, here]),...  1.4 us
    pallas_call x1, Pallas kernels, per_device(): pl.pallas_call(functools.partial(lags_kernel, parts, freq_parts), out_sha...  1.04 us
    pallas_call x1, Pallas kernels, per_device(): pl.pallas_call(functools.partial(table_kernel, hours * hour_parts), out_s...  0.47 us
  transfers between devices with their start and end apart: 6, of which 4 were waited for; matrix products, arithmetic and copies ran while one was open for 0% of the time, Pallas kernels for 2%

profile of v5, /device:TPU:0, one launch (start us, length us, event | category | flops | bytes accessed | tf_op | source)
XLA Modules:
  0.0 23.1 jit_solution(1002248068755430859)
XLA Ops:
  0.0 1.4 %send_slots.1 = (bf16[2,8,16,256]{3,2,1,0:T(8,128)(2,1)S(1)}, bf16[2,8,16,256]{3,2,1,0:T(8,128)(2,1)S(1)}, bf16[2,8,16,256]{3,2,1,0:T(8,128)(2,1)S(1)}, bf16[2,8,16,256]{3,2,1,0:T(8,128)(2,1)S(1)}, s32[2,8]{1,0:T(2,128)S(4)}) custom-call(s32[2,8]{1,0:T(2,128)} %bitcast.1, s32[8,128]{1,0:T(8,128)} %uptime_hbm.1, bf16[8,128,2,256]{3,2,1,0:T(2,128)(2,1)} %spectra_hbm.1), custom_call_target="tpu_custom_call" | custom-call | tf_op jit(solution)/shard_map/send_slots/pallas_call | solution.py:253
  1.4 5.1 %collective-permute-start = (bf16[2,8,16,256]{3,2,1,0:T(8,128)(2,1)S(1)}, bf16[2,8,16,256]{3,2,1,0:T(8,128)(2,1)S(1)}, u32[]{:S(2)}, u32[]{:S(2)}) collective-permute-start(bf16[2,8,16,256]{3,2,1,0:T(8,128)(2,1)S(1)} %get-tuple-element.19), channel_id=1, source_target_pairs={{0,12},{4,8},{8,0},{12,4},{1,13},{5,9},{9,1},{13,5},{2,14},{6,10},... | collective-permute-start | bytes 393224 | tf_op jit(solution)/shard_map/ppermute | solution.py:267
  6.5 0.0 collective-permute-start.1
  6.5 0.9 %collective-permute-start.2 = (bf16[2,8,16,256]{3,2,1,0:T(8,128)(2,1)S(1)}, bf16[2,8,16,256]{3,2,1,0:T(8,128)(2,1)S(1)}, u32[]{:S(2)}, u32[]{:S(2)}) collective-permute-start(bf16[2,8,16,256]{3,2,1,0:T(8,128)(2,1)S(1)} %get-tuple-element.21), channel_id=1, source_target_pairs={{0,4},{4,0},{8,12},{12,8},{1,5},{5,1},{9,13},{13,9},{2,6},{6,2},{1... | collective-permute-start | bytes 393224 | tf_op jit(solution)/shard_map/ppermute | solution.py:267
  7.4 8.1 %collective-permute-done.refs_0_ = bf16[2,8,16,256]{3,2,1,0:T(8,128)(2,1)S(1)} collective-permute-done((bf16[2,8,16,256]{3,2,1,0:T(8,128)(2,1)S(1)}, bf16[2,8,16,256]{3,2,1,0:T(8,128)(2,1)S(1)}, u32[]{:S(2)}, u32[]{:S(2)}) %collective-permute-start) | collective-permute-done | bytes 131104 | tf_op jit(solution)/shard_map/ppermute | solution.py:267
  15.5 0.0 collective-permute-done.1.refs_1_
  15.5 0.4 %collective-permute-done.2.refs_2_ = bf16[2,8,16,256]{3,2,1,0:T(8,128)(2,1)S(1)} collective-permute-done((bf16[2,8,16,256]{3,2,1,0:T(8,128)(2,1)S(1)}, bf16[2,8,16,256]{3,2,1,0:T(8,128)(2,1)S(1)}, u32[]{:S(2)}, u32[]{:S(2)}) %collective-permute-start.2) | collective-permute-done | bytes 131104 | tf_op jit(solution)/shard_map/ppermute | solution.py:267
  15.9 0.4 %cross.1 = (f32[2,32,256]{2,1,0:T(8,128)S(1)}, f32[2,32,256]{2,1,0:T(8,128)S(1)}, f32[2,32,256]{2,1,0:T(8,128)S(1)}, f32[2,32,256]{2,1,0:T(8,128)S(1)}) custom-call(s32[2,8]{1,0:T(2,128)S(4)} %get-tuple-element.16.wanted_ref.pairs_ref, bf16[2,8,16,256]{3,2,1,0:T(8,128)(2,1)S(1)} %collective-permute-done.refs_0_, ...), custom_call_target="tpu_custom_call" | custom-call | tf_op jit(solution)/shard_map/cross/pallas_call | solution.py:283
  16.3 0.1 collective-permute-start.3
  16.4 1.6 %collective-permute-start.4 = (f32[2,32,256]{2,1,0:T(8,128)S(1)}, f32[2,32,256]{2,1,0:T(8,128)S(1)}, u32[]{:S(2)}, u32[]{:S(2)}) collective-permute-start(f32[2,32,256]{2,1,0:T(8,128)S(1)} %get-tuple-element.25), channel_id=1, source_target_pairs={{0,2},{1,3},{2,0},{3,1},{4,6},{5,7},{6,4},{7,5},{8,10},{9,11},{10,... | collective-permute-start | bytes 196616 | tf_op jit(solution)/shard_map/ppermute | solution.py:32
  18.0 0.3 %collective-permute-start.5 = (f32[2,32,256]{2,1,0:T(8,128)S(1)}, f32[2,32,256]{2,1,0:T(8,128)S(1)}, u32[]{:S(2)}, u32[]{:S(2)}) collective-permute-start(f32[2,32,256]{2,1,0:T(8,128)S(1)} %get-tuple-element.26), channel_id=1, source_target_pairs={{0,3},{1,2},{2,1},{3,0},{4,7},{5,6},{6,5},{7,4},{8,11},{9,10},{10,... | collective-permute-start | bytes 196616 | tf_op jit(solution)/shard_map/ppermute | solution.py:32
  18.3 0.5 %band_table.1 = (bf16[2,512,256]{2,1,0:T(8,128)(2,1)S(1)}, bf16[2,512,256]{2,1,0:T(8,128)(2,1)S(1)}) custom-call(s32[2,8]{1,0:T(2,128)S(4)} %get-tuple-element.16.wanted_ref.pairs_ref), custom_call_target="tpu_custom_call" | custom-call | flops 5000000 | bytes 2000000 | tf_op jit(solution)/shard_map/band_table/pallas_call | solution.py:273
  18.7 0.0 collective-permute-done.3.refs_1_
  18.8 2.2 %collective-permute-done.4.refs_2_ = f32[2,32,256]{2,1,0:T(8,128)S(1)} collective-permute-done((f32[2,32,256]{2,1,0:T(8,128)S(1)}, f32[2,32,256]{2,1,0:T(8,128)S(1)}, u32[]{:S(2)}, u32[]{:S(2)}) %collective-permute-start.4) | collective-permute-done | bytes 65568 | tf_op jit(solution)/shard_map/ppermute | solution.py:32
  20.9 1.1 %collective-permute-done.5.refs_3_ = f32[2,32,256]{2,1,0:T(8,128)S(1)} collective-permute-done((f32[2,32,256]{2,1,0:T(8,128)S(1)}, f32[2,32,256]{2,1,0:T(8,128)S(1)}, u32[]{:S(2)}, u32[]{:S(2)}) %collective-permute-start.5) | collective-permute-done | bytes 65568 | tf_op jit(solution)/shard_map/ppermute | solution.py:32
  22.1 1.0 %lags.1 = f32[32,1024]{1,0:T(8,128)} custom-call(bf16[2,512,256]{2,1,0:T(8,128)(2,1)S(1)} %get-tuple-element.17.high_ref, bf16[2,512,256]{2,1,0:T(8,128)(2,1)S(1)} %get-tuple-element.18.low_ref, f32[2,32,256]{2,1,0:T(8,128)S(1)} %get-tuple-element.23.refs_0_, f32[2,32,256]{2,1,0:T(8,128)S(1)} %collective-permute-done.3.refs_1_, ...), custom_call_target="tpu_custom_call" | custom-call | tf_op jit(solution)/shard_map/lags/pallas_call | solution.py:298
Async XLA Ops:
  1.4 14.1 %collective-permute-start = (bf16[2,8,16,256]{3,2,1,0:T(8,128)(2,1)S(1)}, bf16[2,8,16,256]{3,2,1,0:T(8,128)(2,1)S(1)}, u32[]{:S(2)}, u32[]{:S(2)}) collective-permute-start(bf16[2,8,16,256]{3,2,1,0:T(8,128)(2,1)S(1)} %get-tuple-element.19), channel_id=1, source_target_pairs={{0,12},{4,8},{8,0},{12,4},{1,13},{5,9},{9,1},{13,5},{2,14},{6,10},... | collective-permute-start | bytes 393224 | tf_op jit(solution)/shard_map/ppermute | solution.py:267
  6.5 9.0 %collective-permute-start.1 = (bf16[2,8,16,256]{3,2,1,0:T(8,128)(2,1)S(1)}, bf16[2,8,16,256]{3,2,1,0:T(8,128)(2,1)S(1)}, u32[]{:S(2)}, u32[]{:S(2)}) collective-permute-start(bf16[2,8,16,256]{3,2,1,0:T(8,128)(2,1)S(1)} %get-tuple-element.20), channel_id=1, source_target_pairs={{0,8},{4,12},{8,4},{12,0},{1,9},{5,13},{9,5},{13,1},{2,10},{6,14},... | collective-permute-start | bytes 393224 | tf_op jit(solution)/shard_map/ppermute | solution.py:267
  6.5 9.4 %collective-permute-start.2 = (bf16[2,8,16,256]{3,2,1,0:T(8,128)(2,1)S(1)}, bf16[2,8,16,256]{3,2,1,0:T(8,128)(2,1)S(1)}, u32[]{:S(2)}, u32[]{:S(2)}) collective-permute-start(bf16[2,8,16,256]{3,2,1,0:T(8,128)(2,1)S(1)} %get-tuple-element.21), channel_id=1, source_target_pairs={{0,4},{4,0},{8,12},{12,8},{1,5},{5,1},{9,13},{13,9},{2,6},{6,2},{1... | collective-permute-start | bytes 393224 | tf_op jit(solution)/shard_map/ppermute | solution.py:267
  16.3 2.4 %collective-permute-start.3 = (f32[2,32,256]{2,1,0:T(8,128)S(1)}, f32[2,32,256]{2,1,0:T(8,128)S(1)}, u32[]{:S(2)}, u32[]{:S(2)}) collective-permute-start(f32[2,32,256]{2,1,0:T(8,128)S(1)} %get-tuple-element.24), channel_id=1, source_target_pairs={{0,1},{1,0},{2,3},{3,2},{4,5},{5,4},{6,7},{7,6},{8,9},{9,8},{10,11... | collective-permute-start | bytes 196616 | tf_op jit(solution)/shard_map/ppermute | solution.py:32
  16.4 4.5 %collective-permute-start.4 = (f32[2,32,256]{2,1,0:T(8,128)S(1)}, f32[2,32,256]{2,1,0:T(8,128)S(1)}, u32[]{:S(2)}, u32[]{:S(2)}) collective-permute-start(f32[2,32,256]{2,1,0:T(8,128)S(1)} %get-tuple-element.25), channel_id=1, source_target_pairs={{0,2},{1,3},{2,0},{3,1},{4,6},{5,7},{6,4},{7,5},{8,10},{9,11},{10,... | collective-permute-start | bytes 196616 | tf_op jit(solution)/shard_map/ppermute | solution.py:32
  18.0 4.0 %collective-permute-start.5 = (f32[2,32,256]{2,1,0:T(8,128)S(1)}, f32[2,32,256]{2,1,0:T(8,128)S(1)}, u32[]{:S(2)}, u32[]{:S(2)}) collective-permute-start(f32[2,32,256]{2,1,0:T(8,128)S(1)} %get-tuple-element.26), channel_id=1, source_target_pairs={{0,3},{1,2},{2,1},{3,0},{4,7},{5,6},{6,5},{7,4},{8,11},{9,10},{10,... | collective-permute-start | bytes 196616 | tf_op jit(solution)/shard_map/ppermute | solution.py:32

commit v6 on v5

--- a/solution.py
+++ b/solution.py
@@ -197,41 +197,42 @@
                 out_refs[distance][1, pl.ds(s * SB, SB), lanes] = imag
 
 
-def lags_kernel(parts, freq_parts, high_ref, low_ref, *refs):
-    part_refs, out_ref = refs[:-1], refs[-1]
-    own = lax.axis_index("freq")
-    count = out_ref.shape[0]
-    chunks = part_refs[0].shape[2] // LANES
-    phase = lax.broadcasted_iota(jnp.int32, (count, LANES), 1) % 4
-    total = None
-    for c in range(freq_parts):
-        highs, lows = [], []
-        for chunk in range(chunks):
-            lanes = pl.ds(chunk * LANES, LANES)
-            cross = part_refs[c][:, :, lanes]
-            for x in range(1, parts // freq_parts):
-                cross = cross + part_refs[x * freq_parts + c][:, :, lanes]
-            real, imag = cross[0], cross[1]
-            turned = []
-            for q in range(4):
-                step = (phase * q) % 4
-                re = jnp.where(step % 2 == 0, real, imag)
-                im = jnp.where(step % 2 == 0, imag, real)
-                re = jnp.where((step == 1) | (step == 2), -re, re)
-                im = jnp.where((step == 2) | (step == 3), -im, im)
-                turned.append(jnp.concatenate([re, im], axis=1))
-            turned = jnp.concatenate(turned, axis=0)
-            high = turned.astype(jnp.bfloat16)
-            highs.append(high)
-            lows.append((turned - high.astype(jnp.float32)).astype(jnp.bfloat16))
-        high, low = jnp.concatenate(highs, axis=1), jnp.concatenate(lows, axis=1)
-        both = jnp.concatenate([high, low], axis=0)
-        by_high = jnp.dot(both, high_ref[own ^ c], preferred_element_type=jnp.float32)
-        by_low = jnp.dot(high, low_ref[own ^ c], preferred_element_type=jnp.float32)
-        term = by_high[: 4 * count] + (by_high[4 * count :] + by_low)
-        total = term if total is None else total + term
-    for q in range(4):
-        out_ref[:, q * QUARTER : (q + 1) * QUARTER] = total[q * count : (q + 1) * count]
+def lags_kernel(c, count, high_ref, low_ref, *refs):
+    part_refs, before_refs, out_ref = refs[:count], refs[count:-1], refs[-1]
+    table = lax.axis_index("freq") ^ c
+    _, pairs, freq_loc = part_refs[0].shape
+    phase = lax.broadcasted_iota(jnp.int32, (pairs, LANES), 1) % 4
+    highs, lows = [], []
+    for first in range(0, freq_loc, LANES):
+        lanes = pl.ds(first, LANES)
+        cross = part_refs[0][:, :, lanes]
+        for part_ref in part_refs[1:]:
+            cross = cross + part_ref[:, :, lanes]
+        real, imag = cross[0], cross[1]
+        turned = []
+        for q in range(4):
+            step = (phase * q) % 4
+            re = jnp.where(step % 2 == 0, real, imag)
+            im = jnp.where(step % 2 == 0, imag, real)
+            re = jnp.where((step == 1) | (step == 2), -re, re)
+            im = jnp.where((step == 2) | (step == 3), -im, im)
+            turned.append(jnp.concatenate([re, im], axis=1))
+        turned = jnp.concatenate(turned, axis=0)
+        high = turned.astype(jnp.bfloat16)
+        highs.append(high)
+        lows.append((turned - high.astype(jnp.float32)).astype(jnp.bfloat16))
+    high, low = jnp.concatenate(highs, axis=1), jnp.concatenate(lows, axis=1)
+    both = jnp.concatenate([high, low], axis=0)
+    by_high = jnp.dot(both, high_ref[table], preferred_element_type=jnp.float32)
+    by_low = jnp.dot(high, low_ref[table], preferred_element_type=jnp.float32)
+    total = by_high[: 4 * pairs] + (by_high[4 * pairs :] + by_low)
+    for before_ref in before_refs:
+        total = total + before_ref[...]
+    if out_ref.shape == total.shape:
+        out_ref[...] = total
+    else:
+        for q in range(4):
+            out_ref[:, q * QUARTER : (q + 1) * QUARTER] = total[q * pairs : (q + 1) * pairs]
 
 
 def per_device(sizes, spectra, uptime, pair_blocks):
@@ -295,14 +296,21 @@
         exchange(cross[distance], ("hour", "freq"), parts, distance) for distance in range(1, parts)
     ]
 
-    return pl.pallas_call(
-        functools.partial(lags_kernel, parts, freq_parts),
-        out_shape=jax.ShapeDtypeStruct((part_pairs, L), jnp.float32),
-        in_specs=[vmem] * (2 + parts),
-        out_specs=vmem,
-        compiler_params=limit,
-        name="lags",
-    )(high, low, *summed)
+    lags = []
+    for c in range(freq_parts):
+        shares = summed[c::freq_parts]
+        last = c == freq_parts - 1
+        lags = pl.pallas_call(
+            functools.partial(lags_kernel, c, len(shares)),
+            out_shape=[
+                jax.ShapeDtypeStruct((part_pairs, L) if last else (4 * part_pairs, QUARTER), jnp.float32)
+            ],
+            in_specs=[vmem] * (2 + len(shares) + len(lags)),
+            out_specs=[vmem],
+            compiler_params=limit,
+            name="lags",
+        )(high, low, *shares, *lags)
+    return lags[0]
 
 
 def solution(mesh):

time: 23.2 us -> 22.8 us (0.983)
  waiting for transfers between devices: 11.8 us -> 10.9 us
  starting transfers between devices: 7.93 us -> 8.21 us
    ppermute x3, waiting for transfers between devices: 3.31 us -> 2.38 us  [exchange(): return lax.ppermute(x, axes, [(i, i ^ distance) for i in range(size)])]
    ppermute x3, starting transfers between devices: 1.93 us -> 2.21 us  [exchange(): return lax.ppermute(x, axes, [(i, i ^ distance) for i in range(size)])]
    pallas_call x1 -> x2, Pallas kernels: 1.04 us -> 1.21 us  [per_device(): pl.pallas_call(functools.partial(lags_kernel, c, len(shares)), out_shape=...]
  transfers between devices with their start and end apart: 6 -> 6, of which waited for: 4 -> 4; matrix products, arithmetic and copies ran while one was open for 0% -> 0% of each run, Pallas kernels for 2% -> 3%
where the time goes in v6:
time: 22.8 us; the launch traced here: 22.6 us
  waiting for transfers between devices  10.9 us (48%)
  starting transfers between devices  8.21 us (36%)
  Pallas kernels  3.46 us (15%)
    ppermute x3, waiting for transfers between devices, per_device(): lax.ppermute(slots, 'stn', [*enumerate(targets)])  8.52 us
    ppermute x3, starting transfers between devices, per_device(): lax.ppermute(slots, 'stn', [*enumerate(targets)])  6 us
    ppermute x3, waiting for transfers between devices, exchange(): return lax.ppermute(x, axes, [(i, i ^ distance) for i in range(size)])  2.38 us
    ppermute x3, starting transfers between devices, exchange(): return lax.ppermute(x, axes, [(i, i ^ distance) for i in range(size)])  2.21 us
    pallas_call x1, Pallas kernels, per_device(): pl.pallas_call(functools.partial(send_kernel, readers, [*rounds, here]),...  1.4 us
    pallas_call x2, Pallas kernels, per_device(): pl.pallas_call(functools.partial(lags_kernel, c, len(shares)), out_shape=...  1.21 us
    pallas_call x1, Pallas kernels, per_device(): pl.pallas_call(functools.partial(table_kernel, hours * hour_parts), out_s...  0.47 us
  transfers between devices with their start and end apart: 6, of which 4 were waited for; matrix products, arithmetic and copies ran while one was open for 0% of the time, Pallas kernels for 3%

profile of v6, /device:TPU:0, one launch (start us, length us, event | category | flops | bytes accessed | tf_op | source)
XLA Modules:
  0.0 22.6 jit_solution(16730772615147990743)
XLA Ops:
  0.0 1.4 %send_slots.1 = (bf16[2,8,16,256]{3,2,1,0:T(8,128)(2,1)S(1)}, bf16[2,8,16,256]{3,2,1,0:T(8,128)(2,1)S(1)}, bf16[2,8,16,256]{3,2,1,0:T(8,128)(2,1)S(1)}, bf16[2,8,16,256]{3,2,1,0:T(8,128)(2,1)S(1)}, s32[2,8]{1,0:T(2,128)S(4)}) custom-call(s32[2,8]{1,0:T(2,128)} %bitcast.1, s32[8,128]{1,0:T(8,128)} %uptime_hbm.1, bf16[8,128,2,256]{3,2,1,0:T(2,128)(2,1)} %spectra_hbm.1), custom_call_target="tpu_custom_call" | custom-call | tf_op jit(solution)/shard_map/send_slots/pallas_call | solution.py:254
  1.4 5.1 %collective-permute-start = (bf16[2,8,16,256]{3,2,1,0:T(8,128)(2,1)S(1)}, bf16[2,8,16,256]{3,2,1,0:T(8,128)(2,1)S(1)}, u32[]{:S(2)}, u32[]{:S(2)}) collective-permute-start(bf16[2,8,16,256]{3,2,1,0:T(8,128)(2,1)S(1)} %get-tuple-element.19), channel_id=1, source_target_pairs={{0,12},{4,8},{8,0},{12,4},{1,13},{5,9},{9,1},{13,5},{2,14},{6,10},... | collective-permute-start | bytes 393224 | tf_op jit(solution)/shard_map/ppermute | solution.py:268
  6.5 0.0 collective-permute-start.1
  6.5 0.9 %collective-permute-start.2 = (bf16[2,8,16,256]{3,2,1,0:T(8,128)(2,1)S(1)}, bf16[2,8,16,256]{3,2,1,0:T(8,128)(2,1)S(1)}, u32[]{:S(2)}, u32[]{:S(2)}) collective-permute-start(bf16[2,8,16,256]{3,2,1,0:T(8,128)(2,1)S(1)} %get-tuple-element.21), channel_id=1, source_target_pairs={{0,4},{4,0},{8,12},{12,8},{1,5},{5,1},{9,13},{13,9},{2,6},{6,2},{1... | collective-permute-start | bytes 393224 | tf_op jit(solution)/shard_map/ppermute | solution.py:268
  7.4 8.1 %collective-permute-done.refs_0_ = bf16[2,8,16,256]{3,2,1,0:T(8,128)(2,1)S(1)} collective-permute-done((bf16[2,8,16,256]{3,2,1,0:T(8,128)(2,1)S(1)}, bf16[2,8,16,256]{3,2,1,0:T(8,128)(2,1)S(1)}, u32[]{:S(2)}, u32[]{:S(2)}) %collective-permute-start) | collective-permute-done | bytes 131104 | tf_op jit(solution)/shard_map/ppermute | solution.py:268
  15.5 0.0 collective-permute-done.1.refs_1_
  15.5 0.4 %collective-permute-done.2.refs_2_ = bf16[2,8,16,256]{3,2,1,0:T(8,128)(2,1)S(1)} collective-permute-done((bf16[2,8,16,256]{3,2,1,0:T(8,128)(2,1)S(1)}, bf16[2,8,16,256]{3,2,1,0:T(8,128)(2,1)S(1)}, u32[]{:S(2)}, u32[]{:S(2)}) %collective-permute-start.2) | collective-permute-done | bytes 131104 | tf_op jit(solution)/shard_map/ppermute | solution.py:268
  15.9 0.4 %cross.1 = (f32[2,32,256]{2,1,0:T(8,128)S(1)}, f32[2,32,256]{2,1,0:T(8,128)S(1)}, f32[2,32,256]{2,1,0:T(8,128)S(1)}, f32[2,32,256]{2,1,0:T(8,128)S(1)}) custom-call(s32[2,8]{1,0:T(2,128)S(4)} %get-tuple-element.16.wanted_ref.pairs_ref, bf16[2,8,16,256]{3,2,1,0:T(8,128)(2,1)S(1)} %collective-permute-done.refs_0_, ...), custom_call_target="tpu_custom_call" | custom-call | tf_op jit(solution)/shard_map/cross/pallas_call | solution.py:284
  16.3 1.6 %collective-permute-start.5 = (f32[2,32,256]{2,1,0:T(8,128)S(1)}, f32[2,32,256]{2,1,0:T(8,128)S(1)}, u32[]{:S(2)}, u32[]{:S(2)}) collective-permute-start(f32[2,32,256]{2,1,0:T(8,128)S(1)} %get-tuple-element.26), channel_id=1, source_target_pairs={{0,2},{1,3},{2,0},{3,1},{4,6},{5,7},{6,4},{7,5},{8,10},{9,11},{10,... | collective-permute-start | bytes 196616 | tf_op jit(solution)/shard_map/ppermute | solution.py:32
  17.9 0.0 collective-permute-start.3
  17.9 0.6 %collective-permute-start.4 = (f32[2,32,256]{2,1,0:T(8,128)S(1)}, f32[2,32,256]{2,1,0:T(8,128)S(1)}, u32[]{:S(2)}, u32[]{:S(2)}) collective-permute-start(f32[2,32,256]{2,1,0:T(8,128)S(1)} %get-tuple-element.24), channel_id=1, source_target_pairs={{0,3},{1,2},{2,1},{3,0},{4,7},{5,6},{6,5},{7,4},{8,11},{9,10},{10,... | collective-permute-start | bytes 196616 | tf_op jit(solution)/shard_map/ppermute | solution.py:32
  18.5 0.5 %band_table.1 = (bf16[2,512,256]{2,1,0:T(8,128)(2,1)S(1)}, bf16[2,512,256]{2,1,0:T(8,128)(2,1)S(1)}) custom-call(s32[2,8]{1,0:T(2,128)S(4)} %get-tuple-element.16.wanted_ref.pairs_ref), custom_call_target="tpu_custom_call" | custom-call | flops 5000000 | bytes 2000000 | tf_op jit(solution)/shard_map/band_table/pallas_call | solution.py:274
  19.0 1.6 %collective-permute-done.5.refs_1_ = f32[2,32,256]{2,1,0:T(8,128)S(1)} collective-permute-done((f32[2,32,256]{2,1,0:T(8,128)S(1)}, f32[2,32,256]{2,1,0:T(8,128)S(1)}, u32[]{:S(2)}, u32[]{:S(2)}) %collective-permute-start.5) | collective-permute-done | bytes 65568 | tf_op jit(solution)/shard_map/ppermute | solution.py:32
  20.6 0.3 %lags.2.refs_2_ = f32[128,256]{1,0:T(8,128)S(1)} custom-call(bf16[2,512,256]{2,1,0:T(8,128)(2,1)S(1)} %get-tuple-element.17.high_ref, bf16[2,512,256]{2,1,0:T(8,128)(2,1)S(1)} %get-tuple-element.18.low_ref, f32[2,32,256]{2,1,0:T(8,128)S(1)} %get-tuple-element.25.refs_0_, f32[2,32,256]{2,1,0:T(8,128)S(1)} %collective-permute-done.5.refs_1_), custom_call_target="tpu_custom_call" | custom-call | tf_op jit(solution)/shard_map/lags/pallas_call | solution.py:303
  20.9 0.0 collective-permute-done.3.refs_0_
  20.9 0.7 %collective-permute-done.4.refs_1_ = f32[2,32,256]{2,1,0:T(8,128)S(1)} collective-permute-done((f32[2,32,256]{2,1,0:T(8,128)S(1)}, f32[2,32,256]{2,1,0:T(8,128)S(1)}, u32[]{:S(2)}, u32[]{:S(2)}) %collective-permute-start.4) | collective-permute-done | bytes 65568 | tf_op jit(solution)/shard_map/ppermute | solution.py:32
  21.7 0.9 %lags.3 = f32[32,1024]{1,0:T(8,128)} custom-call(bf16[2,512,256]{2,1,0:T(8,128)(2,1)S(1)} %get-tuple-element.17.high_ref, bf16[2,512,256]{2,1,0:T(8,128)(2,1)S(1)} %get-tuple-element.18.low_ref, f32[2,32,256]{2,1,0:T(8,128)S(1)} %collective-permute-done.3.refs_0_, f32[2,32,256]{2,1,0:T(8,128)S(1)} %collective-permute-done.4.refs_1_, f32[128,256]{1,0:T(8,128)S(1)} %lags.2.refs_2_), custom_call_target="tpu_custom_call" | custom-call | tf_op jit(solution)/shard_map/lags/pallas_call | solution.py:303
Async XLA Ops:
  1.4 14.1 %collective-permute-start = (bf16[2,8,16,256]{3,2,1,0:T(8,128)(2,1)S(1)}, bf16[2,8,16,256]{3,2,1,0:T(8,128)(2,1)S(1)}, u32[]{:S(2)}, u32[]{:S(2)}) collective-permute-start(bf16[2,8,16,256]{3,2,1,0:T(8,128)(2,1)S(1)} %get-tuple-element.19), channel_id=1, source_target_pairs={{0,12},{4,8},{8,0},{12,4},{1,13},{5,9},{9,1},{13,5},{2,14},{6,10},... | collective-permute-start | bytes 393224 | tf_op jit(solution)/shard_map/ppermute | solution.py:268
  6.5 9.0 %collective-permute-start.1 = (bf16[2,8,16,256]{3,2,1,0:T(8,128)(2,1)S(1)}, bf16[2,8,16,256]{3,2,1,0:T(8,128)(2,1)S(1)}, u32[]{:S(2)}, u32[]{:S(2)}) collective-permute-start(bf16[2,8,16,256]{3,2,1,0:T(8,128)(2,1)S(1)} %get-tuple-element.20), channel_id=1, source_target_pairs={{0,8},{4,12},{8,4},{12,0},{1,9},{5,13},{9,5},{13,1},{2,10},{6,14},... | collective-permute-start | bytes 393224 | tf_op jit(solution)/shard_map/ppermute | solution.py:268
  6.5 9.4 %collective-permute-start.2 = (bf16[2,8,16,256]{3,2,1,0:T(8,128)(2,1)S(1)}, bf16[2,8,16,256]{3,2,1,0:T(8,128)(2,1)S(1)}, u32[]{:S(2)}, u32[]{:S(2)}) collective-permute-start(bf16[2,8,16,256]{3,2,1,0:T(8,128)(2,1)S(1)} %get-tuple-element.21), channel_id=1, source_target_pairs={{0,4},{4,0},{8,12},{12,8},{1,5},{5,1},{9,13},{13,9},{2,6},{6,2},{1... | collective-permute-start | bytes 393224 | tf_op jit(solution)/shard_map/ppermute | solution.py:268
  16.3 4.3 %collective-permute-start.5 = (f32[2,32,256]{2,1,0:T(8,128)S(1)}, f32[2,32,256]{2,1,0:T(8,128)S(1)}, u32[]{:S(2)}, u32[]{:S(2)}) collective-permute-start(f32[2,32,256]{2,1,0:T(8,128)S(1)} %get-tuple-element.26), channel_id=1, source_target_pairs={{0,2},{1,3},{2,0},{3,1},{4,6},{5,7},{6,4},{7,5},{8,10},{9,11},{10,... | collective-permute-start | bytes 196616 | tf_op jit(solution)/shard_map/ppermute | solution.py:32
  17.9 3.0 %collective-permute-start.3 = (f32[2,32,256]{2,1,0:T(8,128)S(1)}, f32[2,32,256]{2,1,0:T(8,128)S(1)}, u32[]{:S(2)}, u32[]{:S(2)}) collective-permute-start(f32[2,32,256]{2,1,0:T(8,128)S(1)} %get-tuple-element.23), channel_id=1, source_target_pairs={{0,1},{1,0},{2,3},{3,2},{4,5},{5,4},{6,7},{7,6},{8,9},{9,8},{10,11... | collective-permute-start | bytes 196616 | tf_op jit(solution)/shard_map/ppermute | solution.py:32
  17.9 3.7 %collective-permute-start.4 = (f32[2,32,256]{2,1,0:T(8,128)S(1)}, f32[2,32,256]{2,1,0:T(8,128)S(1)}, u32[]{:S(2)}, u32[]{:S(2)}) collective-permute-start(f32[2,32,256]{2,1,0:T(8,128)S(1)} %get-tuple-element.24), channel_id=1, source_target_pairs={{0,3},{1,2},{2,1},{3,0},{4,7},{5,6},{6,5},{7,4},{8,11},{9,10},{10,... | collective-permute-start | bytes 196616 | tf_op jit(solution)/shard_map/ppermute | solution.py:32

commit v7 on v6

--- a/solution.py
+++ b/solution.py
@@ -150,10 +150,10 @@
     return out_cos, out_sin
 
 
-def cross_kernel(rounds, parts, freq_parts, owned, pairs_ref, *refs):
+def cross_kernel(rounds, targets, freq_parts, owned, pairs_ref, *refs):
     readers = len(rounds[0])
     count = len(rounds)
-    slot_refs, out_refs, blocks = refs[:count], refs[count : count + parts], refs[-1]
+    slot_refs, out_refs, blocks = refs[:count], refs[count:-1], refs[-1]
     me = lax.axis_index("stn")
     mine = lax.axis_index("hour") * freq_parts + lax.axis_index("freq")
     reader_blocks = pairs_ref.shape[1] // readers
@@ -162,22 +162,25 @@
     for entry in range(2 * reader_blocks):
         wanted.append(pairs_ref[entry % 2, me * reader_blocks + entry // 2])
     owners = [block // owned for block in wanted]
+    part_rows = out_refs[0].shape[1] // SB
+    first_rows = [(mine ^ distance) * part_rows for distance in targets]
     for entry in range(2 * reader_blocks):
         slot = jnp.int32(0)
         for before in range(entry):
             slot = slot + (owners[before] == owners[entry]).astype(jnp.int32)
         slot = jnp.minimum(slot, CAP - 1)
+        needed = first_rows[0] // SB == entry // 2
+        for first_row in first_rows[1:]:
+            needed = needed | (first_row // SB == entry // 2)
         for slot_ref, sources in zip(slot_refs, rounds, strict=True):
 
-            @pl.when(owners[entry] == pick(sources, me))
+            @pl.when(needed & (owners[entry] == pick(sources, me)))
             def _(entry=entry, slot=slot, slot_ref=slot_ref):
                 values = slot_ref[slot].astype(jnp.float32)
                 for chunk in range(chunks):
                     blocks[entry, chunk] = values[:, :, chunk * LANES : (chunk + 1) * LANES]
 
-    part_rows = out_refs[0].shape[1] // SB
-    for distance in range(parts):
-        first_row = (mine ^ distance) * part_rows
+    for out_ref, first_row in zip(out_refs, first_rows, strict=True):
         pair = first_row // SB
         station = first_row % SB
         for chunk in range(chunks):
@@ -193,8 +196,8 @@
                     first_im = blocks[2 * pair, chunk, h, pl.ds(2 * (station + s) + 1, 1)]
                     real = real + first_re * second_re[h] + first_im * second_im[h]
                     imag = imag + first_im * second_re[h] - first_re * second_im[h]
-                out_refs[distance][0, pl.ds(s * SB, SB), lanes] = real
-                out_refs[distance][1, pl.ds(s * SB, SB), lanes] = imag
+                out_ref[0, pl.ds(s * SB, SB), lanes] = real
+                out_ref[1, pl.ds(s * SB, SB), lanes] = imag
 
 
 def lags_kernel(c, count, high_ref, low_ref, *refs):
@@ -281,20 +284,23 @@
         name="band_table",
     )(pltpu.with_memory_space_constraint(wanted, pltpu.SMEM))
 
-    cross = pl.pallas_call(
-        functools.partial(cross_kernel, [*sources, here], parts, freq_parts, stations // SB),
-        out_shape=[jax.ShapeDtypeStruct((2, part_pairs, freq_loc), jnp.float32)] * parts,
-        in_specs=[smem] + [vmem] * (len(rounds) + 1),
-        out_specs=[vmem] * parts,
-        scratch_shapes=[
-            pltpu.VMEM((2 * reader_blocks, chunks, hours, 2 * SB, LANES), jnp.float32)
-        ],
-        compiler_params=limit,
-        name="cross",
-    )(pltpu.with_memory_space_constraint(wanted, pltpu.SMEM), *arrived, own)
-    summed = [cross[0]] + [
-        exchange(cross[distance], ("hour", "freq"), parts, distance) for distance in range(1, parts)
-    ]
+    summed = [None] * parts
+    for targets in ([*range(1, parts)], [0]):
+        cross = pl.pallas_call(
+            functools.partial(cross_kernel, [*sources, here], targets, freq_parts, stations // SB),
+            out_shape=[jax.ShapeDtypeStruct((2, part_pairs, freq_loc), jnp.float32)] * len(targets),
+            in_specs=[smem] + [vmem] * (len(rounds) + 1),
+            out_specs=[vmem] * len(targets),
+            scratch_shapes=[
+                pltpu.VMEM((2 * reader_blocks, chunks, hours, 2 * SB, LANES), jnp.float32)
+            ],
+            compiler_params=limit,
+            name="cross",
+        )(pltpu.with_memory_space_constraint(wanted, pltpu.SMEM), *arrived, own)
+        for part, distance in zip(cross, targets, strict=True):
+            summed[distance] = (
+                exchange(part, ("hour", "freq"), parts, distance) if distance else part
+            )
 
     lags = []
     for c in range(freq_parts):

time: 22.8 us -> 22.7 us (level)
    ppermute x3, waiting for transfers between devices: 2.38 us -> 2.14 us  [exchange(): return lax.ppermute(x, axes, [(i, i ^ distance) for i in range(size)])]
    pallas_call x1 -> x2, Pallas kernels: 0.38 us -> 0.56 us  [per_device(): pl.pallas_call(functools.partial(cross_kernel, [*sources, here], targets,...]
  transfers between devices with their start and end apart: 6 -> 6, of which waited for: 4 -> 4; matrix products, arithmetic and copies ran while one was open for 0% -> 0% of each run, Pallas kernels for 3% -> 4%
where the time goes in v7:
time: 22.7 us; the launch traced here: 22.6 us
  waiting for transfers between devices  10.7 us (47%)
  starting transfers between devices  8.21 us (36%)
  Pallas kernels  3.65 us (16%)
    ppermute x3, waiting for transfers between devices, per_device(): lax.ppermute(slots, 'stn', [*enumerate(targets)])  8.52 us
    ppermute x3, starting transfers between devices, per_device(): lax.ppermute(slots, 'stn', [*enumerate(targets)])  6 us
    ppermute x3, starting transfers between devices, exchange(): return lax.ppermute(x, axes, [(i, i ^ distance) for i in range(size)])  2.21 us
    ppermute x3, waiting for transfers between devices, exchange(): return lax.ppermute(x, axes, [(i, i ^ distance) for i in range(size)])  2.14 us
    pallas_call x1, Pallas kernels, per_device(): pl.pallas_call(functools.partial(send_kernel, readers, [*rounds, here]),...  1.4 us
    pallas_call x2, Pallas kernels, per_device(): pl.pallas_call(functools.partial(lags_kernel, c, len(shares)), out_shape=...  1.22 us
    pallas_call x2, Pallas kernels, per_device(): pl.pallas_call(functools.partial(cross_kernel, [*sources, here], targets,...  0.56 us
    pallas_call x1, Pallas kernels, per_device(): pl.pallas_call(functools.partial(table_kernel, hours * hour_parts), out_s...  0.47 us
  transfers between devices with their start and end apart: 6, of which 4 were waited for; matrix products, arithmetic and copies ran while one was open for 0% of the time, Pallas kernels for 4%

profile of v7, /device:TPU:0, one launch (start us, length us, event | category | flops | bytes accessed | tf_op | source)
XLA Modules:
  0.0 22.6 jit_solution(5168754306918248724)
XLA Ops:
  0.0 1.4 %send_slots.1 = (bf16[2,8,16,256]{3,2,1,0:T(8,128)(2,1)S(1)}, bf16[2,8,16,256]{3,2,1,0:T(8,128)(2,1)S(1)}, bf16[2,8,16,256]{3,2,1,0:T(8,128)(2,1)S(1)}, bf16[2,8,16,256]{3,2,1,0:T(8,128)(2,1)S(1)}, s32[2,8]{1,0:T(2,128)S(4)}) custom-call(s32[2,8]{1,0:T(2,128)} %bitcast.1, s32[8,128]{1,0:T(8,128)} %uptime_hbm.1, bf16[8,128,2,256]{3,2,1,0:T(2,128)(2,1)} %spectra_hbm.1), custom_call_target="tpu_custom_call" | custom-call | tf_op jit(solution)/shard_map/send_slots/pallas_call | solution.py:257
  1.4 5.1 %collective-permute-start = (bf16[2,8,16,256]{3,2,1,0:T(8,128)(2,1)S(1)}, bf16[2,8,16,256]{3,2,1,0:T(8,128)(2,1)S(1)}, u32[]{:S(2)}, u32[]{:S(2)}) collective-permute-start(bf16[2,8,16,256]{3,2,1,0:T(8,128)(2,1)S(1)} %get-tuple-element.18), channel_id=1, source_target_pairs={{0,12},{4,8},{8,0},{12,4},{1,13},{5,9},{9,1},{13,5},{2,14},{6,10},... | collective-permute-start | bytes 393224 | tf_op jit(solution)/shard_map/ppermute | solution.py:271
  6.5 0.0 collective-permute-start.1
  6.5 0.9 %collective-permute-start.2 = (bf16[2,8,16,256]{3,2,1,0:T(8,128)(2,1)S(1)}, bf16[2,8,16,256]{3,2,1,0:T(8,128)(2,1)S(1)}, u32[]{:S(2)}, u32[]{:S(2)}) collective-permute-start(bf16[2,8,16,256]{3,2,1,0:T(8,128)(2,1)S(1)} %get-tuple-element.20), channel_id=1, source_target_pairs={{0,4},{4,0},{8,12},{12,8},{1,5},{5,1},{9,13},{13,9},{2,6},{6,2},{1... | collective-permute-start | bytes 393224 | tf_op jit(solution)/shard_map/ppermute | solution.py:271
  7.4 8.1 %collective-permute-done.refs_0_ = bf16[2,8,16,256]{3,2,1,0:T(8,128)(2,1)S(1)} collective-permute-done((bf16[2,8,16,256]{3,2,1,0:T(8,128)(2,1)S(1)}, bf16[2,8,16,256]{3,2,1,0:T(8,128)(2,1)S(1)}, u32[]{:S(2)}, u32[]{:S(2)}) %collective-permute-start) | collective-permute-done | bytes 131104 | tf_op jit(solution)/shard_map/ppermute | solution.py:271
  15.5 0.0 collective-permute-done.1.refs_1_
  15.5 0.4 %collective-permute-done.2.refs_2_ = bf16[2,8,16,256]{3,2,1,0:T(8,128)(2,1)S(1)} collective-permute-done((bf16[2,8,16,256]{3,2,1,0:T(8,128)(2,1)S(1)}, bf16[2,8,16,256]{3,2,1,0:T(8,128)(2,1)S(1)}, u32[]{:S(2)}, u32[]{:S(2)}) %collective-permute-start.2) | collective-permute-done | bytes 131104 | tf_op jit(solution)/shard_map/ppermute | solution.py:271
  15.9 0.3 %cross.2 = (f32[2,32,256]{2,1,0:T(8,128)S(1)}, f32[2,32,256]{2,1,0:T(8,128)S(1)}, f32[2,32,256]{2,1,0:T(8,128)S(1)}) custom-call(s32[2,8]{1,0:T(2,128)S(4)} %get-tuple-element.15.wanted_ref.pairs_ref, bf16[2,8,16,256]{3,2,1,0:T(8,128)(2,1)S(1)} %collective-permute-done.refs_0_, bf16[2,8,16,256]{3,2,1,0:T(8,128)(2,1)S(1)} %collective-permute-done.1.refs_1_, ...), custom_call_target="tpu_custom_call" | custom-call | tf_op jit(solution)/shard_map/cross/pallas_call | solution.py:289
  16.3 1.6 %collective-permute-start.5 = (f32[2,32,256]{2,1,0:T(8,128)S(1)}, f32[2,32,256]{2,1,0:T(8,128)S(1)}, u32[]{:S(2)}, u32[]{:S(2)}) collective-permute-start(f32[2,32,256]{2,1,0:T(8,128)S(1)} %get-tuple-element.24), channel_id=1, source_target_pairs={{0,2},{1,3},{2,0},{3,1},{4,6},{5,7},{6,4},{7,5},{8,10},{9,11},{10,... | collective-permute-start | bytes 196616 | tf_op jit(solution)/shard_map/ppermute | solution.py:32
  17.9 0.0 collective-permute-start.3
  17.9 0.6 %collective-permute-start.4 = (f32[2,32,256]{2,1,0:T(8,128)S(1)}, f32[2,32,256]{2,1,0:T(8,128)S(1)}, u32[]{:S(2)}, u32[]{:S(2)}) collective-permute-start(f32[2,32,256]{2,1,0:T(8,128)S(1)} %get-tuple-element.23), channel_id=1, source_target_pairs={{0,3},{1,2},{2,1},{3,0},{4,7},{5,6},{6,5},{7,4},{8,11},{9,10},{10,... | collective-permute-start | bytes 196616 | tf_op jit(solution)/shard_map/ppermute | solution.py:32
  18.5 0.5 %band_table.1 = (bf16[2,512,256]{2,1,0:T(8,128)(2,1)S(1)}, bf16[2,512,256]{2,1,0:T(8,128)(2,1)S(1)}) custom-call(s32[2,8]{1,0:T(2,128)S(4)} %get-tuple-element.15.wanted_ref.pairs_ref), custom_call_target="tpu_custom_call" | custom-call | flops 5000000 | bytes 2000000 | tf_op jit(solution)/shard_map/band_table/pallas_call | solution.py:277
  18.9 0.2 %cross.3.refs_0_ = f32[2,32,256]{2,1,0:T(8,128)S(1)} custom-call(s32[2,8]{1,0:T(2,128)S(4)} %get-tuple-element.15.wanted_ref.pairs_ref, bf16[2,8,16,256]{3,2,1,0:T(8,128)(2,1)S(1)} %collective-permute-done.refs_0_, bf16[2,8,16,256]{3,2,1,0:T(8,128)(2,1)S(1)} %collective-permute-done.1.refs_1_, bf16[2,8,16,256]{3,2,1,0:T(8,128)(2,1)S(1)} %collective-permute-done.2.refs_2_, ...), custom_call_target="tpu_custom_call" | custom-call | tf_op jit(solution)/shard_map/cross/pallas_call | solution.py:289
  19.2 1.4 %collective-permute-done.5.refs_1_ = f32[2,32,256]{2,1,0:T(8,128)S(1)} collective-permute-done((f32[2,32,256]{2,1,0:T(8,128)S(1)}, f32[2,32,256]{2,1,0:T(8,128)S(1)}, u32[]{:S(2)}, u32[]{:S(2)}) %collective-permute-start.5) | collective-permute-done | bytes 65568 | tf_op jit(solution)/shard_map/ppermute | solution.py:32
  20.6 0.3 %lags.2.refs_2_ = f32[128,256]{1,0:T(8,128)S(1)} custom-call(bf16[2,512,256]{2,1,0:T(8,128)(2,1)S(1)} %get-tuple-element.16.high_ref, bf16[2,512,256]{2,1,0:T(8,128)(2,1)S(1)} %get-tuple-element.17.low_ref, f32[2,32,256]{2,1,0:T(8,128)S(1)} %cross.3.refs_0_, f32[2,32,256]{2,1,0:T(8,128)S(1)} %collective-permute-done.5.refs_1_), custom_call_target="tpu_custom_call" | custom-call | tf_op jit(solution)/shard_map/lags/pallas_call | solution.py:309
  20.9 0.0 collective-permute-done.3.refs_0_
  20.9 0.7 %collective-permute-done.4.refs_1_ = f32[2,32,256]{2,1,0:T(8,128)S(1)} collective-permute-done((f32[2,32,256]{2,1,0:T(8,128)S(1)}, f32[2,32,256]{2,1,0:T(8,128)S(1)}, u32[]{:S(2)}, u32[]{:S(2)}) %collective-permute-start.4) | collective-permute-done | bytes 65568 | tf_op jit(solution)/shard_map/ppermute | solution.py:32
  21.6 0.9 %lags.3 = f32[32,1024]{1,0:T(8,128)} custom-call(bf16[2,512,256]{2,1,0:T(8,128)(2,1)S(1)} %get-tuple-element.16.high_ref, bf16[2,512,256]{2,1,0:T(8,128)(2,1)S(1)} %get-tuple-element.17.low_ref, f32[2,32,256]{2,1,0:T(8,128)S(1)} %collective-permute-done.3.refs_0_, f32[2,32,256]{2,1,0:T(8,128)S(1)} %collective-permute-done.4.refs_1_, f32[128,256]{1,0:T(8,128)S(1)} %lags.2.refs_2_), custom_call_target="tpu_custom_call" | custom-call | tf_op jit(solution)/shard_map/lags/pallas_call | solution.py:309
Async XLA Ops:
  1.4 14.1 %collective-permute-start = (bf16[2,8,16,256]{3,2,1,0:T(8,128)(2,1)S(1)}, bf16[2,8,16,256]{3,2,1,0:T(8,128)(2,1)S(1)}, u32[]{:S(2)}, u32[]{:S(2)}) collective-permute-start(bf16[2,8,16,256]{3,2,1,0:T(8,128)(2,1)S(1)} %get-tuple-element.18), channel_id=1, source_target_pairs={{0,12},{4,8},{8,0},{12,4},{1,13},{5,9},{9,1},{13,5},{2,14},{6,10},... | collective-permute-start | bytes 393224 | tf_op jit(solution)/shard_map/ppermute | solution.py:271
  6.5 9.0 %collective-permute-start.1 = (bf16[2,8,16,256]{3,2,1,0:T(8,128)(2,1)S(1)}, bf16[2,8,16,256]{3,2,1,0:T(8,128)(2,1)S(1)}, u32[]{:S(2)}, u32[]{:S(2)}) collective-permute-start(bf16[2,8,16,256]{3,2,1,0:T(8,128)(2,1)S(1)} %get-tuple-element.19), channel_id=1, source_target_pairs={{0,8},{4,12},{8,4},{12,0},{1,9},{5,13},{9,5},{13,1},{2,10},{6,14},... | collective-permute-start | bytes 393224 | tf_op jit(solution)/shard_map/ppermute | solution.py:271
  6.5 9.4 %collective-permute-start.2 = (bf16[2,8,16,256]{3,2,1,0:T(8,128)(2,1)S(1)}, bf16[2,8,16,256]{3,2,1,0:T(8,128)(2,1)S(1)}, u32[]{:S(2)}, u32[]{:S(2)}) collective-permute-start(bf16[2,8,16,256]{3,2,1,0:T(8,128)(2,1)S(1)} %get-tuple-element.20), channel_id=1, source_target_pairs={{0,4},{4,0},{8,12},{12,8},{1,5},{5,1},{9,13},{13,9},{2,6},{6,2},{1... | collective-permute-start | bytes 393224 | tf_op jit(solution)/shard_map/ppermute | solution.py:271
  16.3 4.3 %collective-permute-start.5 = (f32[2,32,256]{2,1,0:T(8,128)S(1)}, f32[2,32,256]{2,1,0:T(8,128)S(1)}, u32[]{:S(2)}, u32[]{:S(2)}) collective-permute-start(f32[2,32,256]{2,1,0:T(8,128)S(1)} %get-tuple-element.24), channel_id=1, source_target_pairs={{0,2},{1,3},{2,0},{3,1},{4,6},{5,7},{6,4},{7,5},{8,10},{9,11},{10,... | collective-permute-start | bytes 196616 | tf_op jit(solution)/shard_map/ppermute | solution.py:32
  17.9 3.0 %collective-permute-start.3 = (f32[2,32,256]{2,1,0:T(8,128)S(1)}, f32[2,32,256]{2,1,0:T(8,128)S(1)}, u32[]{:S(2)}, u32[]{:S(2)}) collective-permute-start(f32[2,32,256]{2,1,0:T(8,128)S(1)} %get-tuple-element.22), channel_id=1, source_target_pairs={{0,1},{1,0},{2,3},{3,2},{4,5},{5,4},{6,7},{7,6},{8,9},{9,8},{10,11... | collective-permute-start | bytes 196616 | tf_op jit(solution)/shard_map/ppermute | solution.py:32
  17.9 3.7 %collective-permute-start.4 = (f32[2,32,256]{2,1,0:T(8,128)S(1)}, f32[2,32,256]{2,1,0:T(8,128)S(1)}, u32[]{:S(2)}, u32[]{:S(2)}) collective-permute-start(f32[2,32,256]{2,1,0:T(8,128)S(1)} %get-tuple-element.23), channel_id=1, source_target_pairs={{0,3},{1,2},{2,1},{3,0},{4,7},{5,6},{6,5},{7,4},{8,11},{9,10},{10,... | collective-permute-start | bytes 196616 | tf_op jit(solution)/shard_map/ppermute | solution.py:32
